TPU v7x, 128 devices: a whole 4x4x4 slice. The times are simulated.
128 devices in a mesh: wide: 16 (over x_lo, z, core), narrow: 8 (over y, x_hi).
Axes of the slice: x: 4 (x_hi: 2, x_lo: 2; x = x_hi * 2 + x_lo), y: 4, z: 4, core: 2. Of those that a mesh axis runs over, the one named last changes fastest.
Arguments:
- cotangent: bfloat16 [16, 128, 128, 128], P('wide', 'narrow'), may hold values from -6 to 6
- decoder_kernel: bfloat16 [512, 9, 16], replicated, may hold values from -0.09375 to 0.09375
- patch_projection_rows: bfloat16 [64, 3072], replicated, may hold values from -1.3 to 1.3
- stored_hidden_state: bfloat16 [4, 4096, 3072], P(None, 'wide'), may hold values from -160 to 160
- output_norm_scale: bfloat16 [4, 3072], replicated, may hold values from -2.5 to 2.5
- output_gate: bfloat16 [4, 3072], replicated, may hold values from -4 to 4
- preactivation_input: bfloat16 [4, 4096, 12288], P(None, 'wide', 'narrow'), may hold values from -6 to 6
- frozen_down_weight: bfloat16 [12288, 3072], P('narrow'), may hold values from -0.0546875 to 0.0546875
- adapter_down_rows: bfloat16 [12288, 64], P('narrow'), may hold values from -0.0546875 to 0.0546875
- adapter_up_rows: bfloat16 [64, 3072], replicated, may hold values from -0.75 to 0.75
Outputs:
- pre_grad: bfloat16 [4, 4096, 12288], P(None, 'wide', 'narrow')
- up_grad: float32 [3072, 64], P('wide')
- down_grad: float32 [12288, 64], P(('narrow', 'wide'))
All inputs are finite; a program needn't handle non-finite values.
Results may differ from a plain program's by a relative error of at most 0.0065.
Values sent between devices are 32-bit elements; how exact they have to be, the bound alone decides.
A program may use at most 128 MiB of HBM per device.

v0:
```python
import jax
import jax.numpy as jnp
from jax import lax
from jax.sharding import PartitionSpec as P

LAT_CH = 16
GROUP = 4


vae_inverse = 1.0 / 0.3611


def gelu_parts(pre):
    m = pre.astype(jnp.float32)
    inner = 0.7978845608 * (m + 0.044715 * m * m * m)
    tval = jnp.tanh(inner)
    value = 0.5 * m * (1.0 + tval)
    slope = 0.5 * (1.0 + tval) + 0.5 * m * (1.0 - tval * tval) * 0.7978845608 * (
        1.0 + 0.134145 * m * m
    )
    return (value, slope)


def local(
    cotangent,
    decoder_kernel,
    patch_projection_rows,
    stored_hidden_state,
    output_norm_scale,
    output_gate,
    preactivation_input,
    frozen_down_weight,
    adapter_down_rows,
    adapter_up_rows,
):
    wide_count = lax.axis_size("wide")
    narrow_count = lax.axis_size("narrow")
    images = wide_count // GROUP
    part = cotangent[0]
    slice_width = part.shape[0]
    side = part.shape[1]
    offset = (
        lax.axis_index("wide") % GROUP * (slice_width * narrow_count)
        + lax.axis_index("narrow") * slice_width
    )
    kernel = lax.dynamic_slice_in_dim(decoder_kernel, offset, slice_width, 0)
    padded = jnp.pad(part, ((0, 0), (1, 1), (1, 1)))
    latent = jnp.zeros((LAT_CH, side, side), jnp.float32)
    for tap in range(9):
        row_tap = tap // 3
        col_tap = tap % 3
        piece = padded[:, 2 - row_tap : 2 - row_tap + side, 2 - col_tap : 2 - col_tap + side]
        latent = latent + jnp.einsum(
            "co,cyx->oyx", kernel[:, tap, :], piece, preferred_element_type=jnp.float32
        )
    band = side // wide_count
    latent = lax.psum(latent, "narrow")
    moved = lax.all_to_all(latent[None], "wide", split_axis=2, concat_axis=0, tiled=True)
    shares = moved.reshape(images, GROUP, LAT_CH, band, side).sum(axis=1)
    shares = shares * vae_inverse
    tok_count = band // 2 * (side // 2)
    patches = shares.reshape(images, LAT_CH, band // 2, 2, side // 2, 2).transpose(0, 2, 4, 1, 3, 5)
    patches = patches.reshape(images, tok_count, LAT_CH * 4).astype(jnp.bfloat16)
    head_grad = jnp.einsum(
        "bsp,pd->bsd", patches, patch_projection_rows, preferred_element_type=jnp.float32
    )
    scaled = head_grad * (1.0 + output_norm_scale.astype(jnp.float32))[:, None, :]
    stored = stored_hidden_state.astype(jnp.float32)
    centered = stored - jnp.mean(stored, axis=2, keepdims=True)
    inv_std = 1.0 / jnp.sqrt(jnp.mean(centered * centered, axis=2, keepdims=True) + 1e-06)
    normed = centered * inv_std
    inner_term = (
        scaled
        - jnp.mean(scaled, axis=2, keepdims=True)
        - normed * jnp.mean(scaled * normed, axis=2, keepdims=True)
    )
    output_gradient = (output_gate.astype(jnp.float32)[:, None, :] * inv_std * inner_term).astype(
        jnp.bfloat16
    )
    value, slope = gelu_parts(preactivation_input)
    hidden_state = value.astype(jnp.bfloat16)
    norm = 1.0 / jnp.sqrt(jnp.float32(images * tok_count * wide_count))
    reduced_partial = jnp.einsum(
        "hiy,yk->hik", hidden_state, adapter_down_rows, preferred_element_type=jnp.float32
    )
    reduced_value = (norm * lax.psum(reduced_partial, "narrow")).astype(jnp.bfloat16)
    backward_pass = jnp.einsum(
        "yqi,pi->yqp", output_gradient, adapter_up_rows, preferred_element_type=jnp.float32
    ).astype(jnp.bfloat16)
    columns = output_gradient
    up_grad = lax.psum_scatter(
        jnp.einsum("bsd,bsr->dr", columns, reduced_value, preferred_element_type=jnp.float32),
        "wide",
        scatter_dimension=0,
        tiled=True,
    )
    columns = hidden_state
    down_grad = lax.psum_scatter(
        norm
        * jnp.einsum("bsf,bsr->fr", columns, backward_pass, preferred_element_type=jnp.float32),
        "wide",
        scatter_dimension=0,
        tiled=True,
    )
    hidden_state_gradient = jnp.einsum(
        "bsd,fd->bsf", output_gradient, frozen_down_weight, preferred_element_type=jnp.float32
    )
    hidden_state_gradient = hidden_state_gradient + jnp.einsum(
        "pzu,lu->pzl", backward_pass, adapter_down_rows, preferred_element_type=jnp.float32
    )
    pre_grad = (hidden_state_gradient * slope).astype(jnp.bfloat16)
    return (pre_grad, up_grad, down_grad)


def solution(mesh):
    placed = (
        P("wide", "narrow", None, None),
        P(),
        P(),
        P(None, "wide", None),
        P(),
        P(),
        P(None, "wide", "narrow"),
        P("narrow", None),
        P("narrow", None),
        P(),
    )
    return jax.shard_map(
        local,
        mesh=mesh,
        in_specs=placed,
        out_specs=(P(None, "wide", "narrow"), P("wide", None), P(("narrow", "wide"), None)),
        check_vma=False,
    )
```

profile of v0, /device:TPU:1, one launch (start us, length us, event | category | flops | bytes accessed | tf_op | source)
XLA Modules:
  0.0 293.7 jit_solution(12306055131662818503)
XLA Ops:
  7.2 1.4 copy.27
  8.7 5.0 %fusion.30 = f32[4,256,64]{1,2,0:T(8,128)} fusion(bf16[1536,64]{0,1:T(8,128)(2,1)} %param.18, bf16[4,256,1536]{2,1,0:T(8,128)(2,1)} %param.16), kind=kOutput, calls=%fused_computation.60 | convolution fusion | flops 217055232 | bytes 3604480 | tf_op jit(solution)/shard_map/hiy,yk->hik/dot_general | solution.py:83
  13.6 1.1 fusion.26
  14.7 1.0 convolution_add_fusion.7
  15.8 1.0 convolution_add_fusion.6
  16.8 1.0 convolution_add_fusion.5
  17.9 1.1 convolution_add_fusion.4
  19.0 1.0 convolution_add_fusion.3
  20.1 1.0 convolution_add_fusion.2
  21.1 1.0 convolution_add_fusion.1
  22.2 2.0 fusion.25
  24.2 3.7 %convert_reduce_fusion = f32[4,256]{1,0:T(4,128)S(1)} fusion(bf16[4,256,3072]{2,1,0:T(8,128)(2,1)} %param.13), kind=kLoop, calls=%fused_computation.8 | loop fusion | flops 6290432 | bytes 6295552 | tf_op jit(solution)/shard_map/reduce_sum | solution.py:69
  27.9 88.0 %all-reduce.4.cloned.1.call-done = (f32[1,16,128,128]{3,1,2,0:T(8,128)}, f32[4,256,64]{1,2,0:T(8,128)}) async-done(((f32[1,16,128,128]{3,1,2,0:T(8,128)}, f32[4,256,64]{1,2,0:T(8,128)}), (f32[1,16,128,128]{3,1,2,0:T(8,128)}, f32[4,256,64]{1,2,0:T(8,128)})) %all-reduce.4.cloned.1.call-update) | async-done | bytes 1310736 | tf_op jit(solution)/shard_map/psum | solution.py:57
  115.9 10.8 %all-to-all-start = ((f32[1,16,128,128]{3,1,0,2:T(8,128)}), f32[1,16,128,128]{3,1,0,2:T(8,128)S(1)}, u32[]{:S(2)}, u32[]{:S(2)}) async-start(f32[1,16,128,128]{3,1,0,2:T(8,128)} %bitcast.98), calls=%async_computation | async-start | bytes 2097152 | tf_op jit(solution)/shard_map/all_to_all | solution.py:58
  127.0 4.6 %fusion.8 = f32[4,256]{1,0:T(4,128)S(1)} fusion(bf16[4,256,3072]{2,1,0:T(8,128)(2,1)} %param.13, f32[4,256]{1,0:T(4,128)S(1)} %broadcast_multiply_fusion.2), kind=kLoop, calls=%fused_computation.17 | loop fusion | flops 12581888 | bytes 6299648 | tf_op jit(solution)/shard_map/reduce_sum | solution.py:70
  132.8 9.8 %all-to-all-done = f32[1,16,128,128]{3,1,0,2:T(8,128)S(1)} async-done(((f32[1,16,128,128]{3,1,0,2:T(8,128)}), f32[1,16,128,128]{3,1,0,2:T(8,128)S(1)}, u32[]{:S(2)}, u32[]{:S(2)}) %all-to-all-start) | async-done | bytes 1048608 | tf_op jit(solution)/shard_map/all_to_all | solution.py:58
  143.2 1.8 copy.20
  145.0 1.2 convert_element_type.46
  146.2 6.5 %multiply_reduce_fusion = (f32[4,256]{1,0:T(4,128)S(1)}, f32[4,256]{1,0:T(4,128)S(1)}, f32[4,256,3072]{2,1,0:T(8,128)S(1)}) fusion(f32[4,3072]{1,0:T(4,128)} %convert_add_fusion.1, f32[4,256]{1,0:T(4,128)S(1)} %add_rsqrt_fusion, f32[4,256]{1,0:T(4,128)S(1)} %broadcast_multiply_fusion.2, bf16[4,256,3072]{2,1,0:T(8,128)(2,1)} %param.13, ...), kind=kOutput, calls=%fused_computation.18 | convolution fusion | flops 424671232 | bytes 19464192 | tf_op jit(solution)/shard_map/bsp,pd->bsd/dot_general | solution.py:64
  152.8 6.1 %fusion.7 = bf16[4,256,3072]{2,1,0:T(8,128)(2,1)S(1)} fusion(bf16[4,256,3072]{2,1,0:T(8,128)(2,1)S(1)} %bitcast.87, f32[4,256,3072]{2,1,0:T(8,128)S(1)} %get-tuple-element.7, f32[4,256]{1,0:T(4,128)S(1)} %get-tuple-element.8, f32[4,256]{1,0:T(4,128)S(1)} %get-tuple-element.9, f32[4,3072]{1,0:T(4,128)S(1)} %copy-done.8, f32[4,256]{1,0:T(4,128)S(1)} %add_rsqrt_fusion, ...), kind=kLoop, calls=%fused_computation.16 | loop fusion | flops 31457280 | bytes 25280512 | tf_op jit(solution)/shard_map/convert_element_type | solution.py:77
  158.9 2.6 copy-done.1
  161.6 2.0 convolution_convert_fusion
  163.7 2.6 fusion.24
  166.3 1.2 copy.23
  167.8 4.1 %fusion.32 = f32[4,256,1536]{2,1,0:T(8,128)} fusion(bf16[4,256,64]{1,2,0:T(8,128)(2,1)S(1)} %convolution_convert_fusion, bf16[1536,64]{0,1:T(8,128)(2,1)S(1)} %copy-done.6), kind=kOutput, calls=%fused_computation.62 | convolution fusion | flops 201326592 | bytes 6619136 | tf_op jit(solution)/shard_map/pzu,lu->pzl/dot_general | solution.py:108
  171.8 0.7 copy-done.2
  172.5 3.8 %convolution_bitcast_fusion = f32[3072,64]{1,0:T(8,128)} fusion(bf16[4,256,3072]{2,1,0:T(8,128)(2,1)S(1)} %copy-done.2, f32[4,256,64]{1,2,0:T(8,128)S(1)} %copy-done.5), kind=kOutput, calls=%fused_computation.32 | convolution fusion | flops 402784256 | bytes 7340032 | tf_op jit(solution)/shard_map/bsd,bsr->dr/dot_general | solution.py:92
  176.3 20.6 %fusion.17 = bf16[4,256,1536]{2,1,0:T(8,128)(2,1)} fusion(bf16[4,256,1536]{2,1,0:T(8,128)(2,1)} %param.16, f32[4,256,1536]{2,1,0:T(8,128)} %fusion.32, bf16[4,256,3072]{2,1,0:T(8,128)(2,1)} %copy-done.1, bf16[1536,3072]{1,0:T(8,128)(2,1)} %param.17), kind=kOutput, calls=%fused_computation.27 | convolution fusion | flops 9696706560 | bytes 28311552 | tf_op jit(solution)/shard_map/bsd,fd->bsf/dot_general | solution.py:105
  197.0 25.1 %reduce-scatter.9.cloned.1.call-done = f32[96,64]{1,0:T(8,128)} async-done(((f32[1536,64]{1,0:T(8,128)}), f32[96,64]{1,0:T(8,128)}) %reduce-scatter.9.cloned.1.call-update) | async-done | bytes 24592
  222.0 1.5 copy.24
  223.5 62.0 %reduce-scatter.7.cloned.1.call-done = f32[192,64]{1,0:T(8,128)} async-done(((f32[3072,64]{1,0:T(8,128)}), f32[192,64]{1,0:T(8,128)}) %reduce-scatter.7.cloned.1.call-update) | async-done | bytes 49168
  285.6 1.6 copy.22
  (41 shorter events, 2.5 us)
Async XLA Ops:
  7.2 139.0 %copy-start = (bf16[64,3072]{1,0:T(8,128)(2,1)S(1)}, bf16[64,3072]{1,0:T(8,128)(2,1)}, u32[]{:S(2)}) copy-start(bf16[64,3072]{1,0:T(8,128)(2,1)} %param.12) | copy-start | bytes 1179652
  7.2 108.7 %all-reduce.4.cloned.1.call-start = ((), (), s32[]{:S(2)}) async-start(), calls=%async_computation.5 | async-start | bytes 2621440 | tf_op jit(solution)/shard_map/psum | solution.py:57
  13.6 4.2 %copy-start.3 = (bf16[1,16,128,128]{3,2,1,0:T(8,128)(2,1)S(1)}, bf16[1,16,128,128]{3,2,1,0:T(8,128)(2,1)}, u32[]{:S(2)}) copy-start(bf16[1,16,128,128]{3,2,1,0:T(8,128)(2,1)} %param.10) | copy-start | bytes 1572868
  24.2 107.3 %copy-start.9 = (bf16[4,3072]{1,0:T(4,128)(2,1)S(1)}, bf16[4,3072]{1,0:T(4,128)(2,1)}, u32[]{:S(2)}) copy-start(bf16[4,3072]{1,0:T(4,128)(2,1)} %param.15) | copy-start | bytes 73732
  24.2 108.0 %copy-start.10 = (bf16[4,3072]{1,0:T(4,128)(2,1)S(1)}, bf16[4,3072]{1,0:T(4,128)(2,1)}, u32[]{:S(2)}) copy-start(bf16[4,3072]{1,0:T(4,128)(2,1)} %param.14) | copy-start | bytes 73732
  115.9 26.7 %all-to-all-start = ((f32[1,16,128,128]{3,1,0,2:T(8,128)}), f32[1,16,128,128]{3,1,0,2:T(8,128)S(1)}, u32[]{:S(2)}, u32[]{:S(2)}) async-start(f32[1,16,128,128]{3,1,0,2:T(8,128)} %bitcast.98), calls=%async_computation | async-start | bytes 2097152 | tf_op jit(solution)/shard_map/all_to_all | solution.py:58
  126.7 95.3 %reduce-scatter.9.cloned.1.call-start = ((), (), s32[]{:S(2)}) async-start(), calls=%async_computation.4 | async-start | bytes 835584
  143.2 9.6 %slice-start = ((s8[6291456]{0:T(1024)(128)(4,1)}), s8[2097152]{0:T(1024)(128)(4,1)S(1)}, s32[]{:S(2)}) async-start(s8[6291456]{0:T(1024)(128)(4,1)} %bitcast.86), calls=%async_computation.6 | async-start | bytes 4194304
  146.2 6.5 %slice-start.1 = ((s8[6291456]{0:T(1024)(128)(4,1)}), s8[4194304]{0:T(1024)(128)(4,1)S(1)}, s32[]{:S(2)}) async-start(s8[6291456]{0:T(1024)(128)(4,1)} %bitcast.86), calls=%async_computation.7 | async-start | bytes 8388608
  146.2 6.5 %copy-start.7 = (f32[4,3072]{1,0:T(4,128)S(1)}, f32[4,3072]{1,0:T(4,128)}, u32[]{:S(2)}) copy-start(f32[4,3072]{1,0:T(4,128)} %convert_element_type.41) | copy-start | bytes 147460
  146.2 6.5 %copy-start.8 = (f32[4,3072]{1,0:T(4,128)S(1)}, f32[4,3072]{1,0:T(4,128)}, u32[]{:S(2)}) copy-start(f32[4,3072]{1,0:T(4,128)} %convert_add_fusion.1) | copy-start | bytes 147460
  152.8 8.8 %copy-start.4 = (bf16[64,3072]{1,0:T(8,128)(2,1)S(1)}, bf16[64,3072]{1,0:T(8,128)(2,1)}, u32[]{:S(2)}) copy-start(bf16[64,3072]{1,0:T(8,128)(2,1)} %param.19) | copy-start | bytes 1179652
  158.9 2.7 copy-start.1
  161.6 2.0 copy-start.11
  163.6 4.1 %copy-start.6 = (bf16[1536,64]{0,1:T(8,128)(2,1)S(1)}, bf16[1536,64]{0,1:T(8,128)(2,1)}, u32[]{:S(2)}) copy-start(bf16[1536,64]{0,1:T(8,128)(2,1)} %param.18) | copy-start | bytes 589828
  166.3 5.6 %copy-start.5 = (f32[4,256,64]{1,2,0:T(8,128)S(1)}, f32[4,256,64]{1,2,0:T(8,128)}, u32[]{:S(2)}) copy-start(f32[4,256,64]{1,2,0:T(8,128)} %get-tuple-element.6) | copy-start | bytes 786436
  167.5 118.1 %reduce-scatter.7.cloned.1.call-start = ((), (), s32[]{:S(2)}) async-start(), calls=%async_computation.3 | async-start | bytes 1671168
  167.8 4.8 %copy-start.2 = (bf16[4,256,3072]{2,1,0:T(8,128)(2,1)S(1)}, bf16[4,256,3072]{2,1,0:T(8,128)(2,1)}, u32[]{:S(2)}) copy-start(bf16[4,256,3072]{2,1,0:T(8,128)(2,1)} %copy-done.1) | copy-start | bytes 18874372
Sparse Core Ops, SparseCore 0:
  24.3 91.5 all-reduce.3
  167.6 54.3 reduce-scatter.8
  224.5 60.9 reduce-scatter.6
where the time goes:
time: 297 us; the launch traced here: 294 us
  waiting for transfers between devices  185 us (62%)
  matrix products  55 us (19%)
  other arithmetic  15.8 us (5%)
  between operations  14.1 us (5%)
  local copies, waits for them, and re-layouts  12.6 us (4%)
  starting transfers between devices  11.3 us (4%)
    psum x1, waiting for transfers between devices, local(): latent = lax.psum(latent, 'narrow')  88 us
    unnamed x5, waiting for transfers between devices  87.2 us
    dot_general x1, matrix products, local(): jnp.einsum('bsd,fd->bsf', output_gradient, frozen_down_weight, preferred_...  20.6 us
    all_to_all x1, starting transfers between devices, local(): lax.all_to_all(latent[None], 'wide', split_axis=2, concat_axis=0, tiled=T...  10.8 us
    dot_general x9, matrix products, local(): jnp.einsum('co,cyx->oyx', kernel[:, tap, :], piece, preferred_element_typ...  10.5 us
    all_to_all x1, waiting for transfers between devices, local(): lax.all_to_all(latent[None], 'wide', split_axis=2, concat_axis=0, tiled=T...  9.77 us
    unnamed x32, local copies, waits for them, and re-layouts  9.12 us
    dot_general x1, matrix products, local(): jnp.einsum('bsp,pd->bsd', patches, patch_projection_rows, preferred_eleme...  6.47 us
  transfers between devices with their start and end apart: 4, of which 4 were waited for; matrix products, arithmetic and copies ran while one was open for 13% of the time, Pallas kernels for 0%

commit v1 on v0

v1 whole, which is shorter than its diff:
```python
import functools

import jax
import jax.numpy as jnp
import numpy as np
from jax import lax
from jax.experimental import pallas as pl
from jax.experimental.pallas import tpu as pltpu
from jax.sharding import PartitionSpec as P

MESH = pl.DeviceIdType.MESH
F32 = jnp.float32
BF16 = jnp.bfloat16
D = 3072
F = 1536
VAE_INVERSE = 1.0 / 0.3611
NORM = 1.0 / 128.0
GELU_A = 0.7978845608
MIB = 1 << 20


def dot_nt(a, b):
    return lax.dot_general(a, b, (((1,), (1,)), ((), ())), preferred_element_type=F32)


def dot_nn(a, b):
    return lax.dot_general(a, b, (((1,), (0,)), ((), ())), preferred_element_type=F32)


def dot_tn(a, b):
    return lax.dot_general(a, b, (((0,), (0,)), ((), ())), preferred_element_type=F32)


def column_taps():
    out = np.zeros((128, 512), np.float32)
    for tap in range(4):
        for q in range(64):
            col = 2 * q - 1 + tap
            if 0 <= col < 128:
                out[col, 128 * tap + q] = 1
                out[col, 128 * tap + 64 + q] = 1
    return out


def kernel_taps():
    out = np.zeros((144, 1024), np.float32)
    for ty in range(4):
        for tx in range(4):
            for i in range(2):
                for j in range(2):
                    dy, dx = i + 2 - ty, j + 2 - tx
                    if 0 <= dy < 3 and 0 <= dx < 3:
                        for o in range(16):
                            out[(3 * dy + dx) * 16 + o, (4 * ty + tx) * 64 + 4 * o + 2 * i + j] = 1
    return out


def conv_kernel(ft_ref, k_ref, s_ref, sel_ref, out_ref, g_ref, w_ref):
    zero = jnp.zeros((16, 128), BF16)
    for tap in range(4):
        g_ref[tap, 0] = zero
        g_ref[tap, 129] = zero

    @pl.loop(0, 8)
    def _(block):
        rows = ft_ref[pl.ds(pl.multiple_of(block * 256, 256), 256), :]
        for tap in range(4):
            moved = dot_nn(rows, s_ref[:, 128 * tap : 128 * tap + 128])
            g_ref[tap, pl.ds(1 + block * 16, 16)] = moved.astype(BF16).reshape(16, 16, 128)

    taps = dot_nn(k_ref[...], sel_ref[...]).astype(BF16)
    for t in range(16):
        w_ref[16 * t : 16 * t + 16, :] = taps[:, 64 * t : 64 * t + 64]
    weights = w_ref[...]
    left = lax.broadcasted_iota(jnp.int32, (16, 128), 1) < 64

    @pl.loop(0, 4)
    def _(quarter):
        for z in range(2):
            for c in range(2):
                for half in range(2):
                    row = 32 * quarter + 16 * z + 8 * c + 4 * half
                    window = [
                        jnp.where(left, g_ref[tx, row + ty], g_ref[tx, row + 2 + ty])
                        for ty in range(4)
                        for tx in range(4)
                    ]
                    out_ref[c, 8 * z + 2 * quarter + half] = dot_tn(weights, jnp.concatenate(window, 0))


def conv(cotangent, kernel):
    ft = cotangent[0].transpose(1, 0, 2).reshape(2048, 128)
    return pl.pallas_call(
        conv_kernel,
        out_shape=jax.ShapeDtypeStruct((2, 16, 64, 128), F32),
        scratch_shapes=[pltpu.VMEM((4, 130, 16, 128), BF16), pltpu.VMEM((256, 64), BF16)],
        compiler_params=pltpu.CompilerParams(vmem_limit_bytes=16 * MIB),
        name="conv",
    )(ft, kernel, jnp.asarray(column_taps(), BF16), jnp.asarray(kernel_taps(), BF16))


def main_kernel(
    part,
    stored,
    pre,
    weight,
    a_ref,
    u_ref,
    p_ref,
    scale_ref,
    gate_ref,
    pre_out,
    up_out,
    down_out,
    own,
    recv_a,
    recv_b,
    red,
    recv_c,
    low_part,
    recv_l,
    red_l,
    recv_m,
    ubuf,
    recv_u,
    red_u,
    recv_e,
    dbuf,
    recv_d,
    stored_v,
    pre_v,
    weight_v,
    zp,
    xw,
    hid,
    slope,
    nz,
    meanb,
    invb,
    vbt,
    ikcol,
    ltile,
    backt,
    klt,
    at_ref,
    gate_v,
    scale_v,
    sem_local,
    sem_pre,
    sem_stored,
    sem_weight,
    sem_out,
    send_a,
    got_a,
    send_b,
    got_b,
    send_c,
    got_c,
    send_l,
    got_l,
    send_m,
    got_m,
    send_u,
    got_u,
    send_e,
    got_e,
    send_d,
    got_d,
):
    w = lax.axis_index("wide")
    n = lax.axis_index("narrow")
    img = lax.div(w, 4)
    grp = lax.rem(w, 4)
    core = lax.rem(w, 2)
    me_b = lax.div(grp, 2) * 8 + n
    c_wide = 4 * lax.div(n, 2) + grp
    e_wide = 2 * n + lax.div(w, 8)
    c_self = c_wide == w
    e_self = e_wide == w

    own_copy = pltpu.make_async_copy(part.at[core], own, sem_local.at[0])
    own_copy.start()

    def pre_copy(i):
        return pltpu.make_async_copy(pre.at[i], pre_v.at[i], sem_pre.at[i])

    def stored_copy(i):
        return pltpu.make_async_copy(stored.at[i], stored_v.at[i], sem_stored.at[i])

    def weight_copy(j):
        rows = pl.ds(pl.multiple_of(j * 256, 256), 256)
        return pltpu.make_async_copy(weight.at[rows], weight_v.at[rows], sem_weight.at[j])

    def out_copy(i):
        return pltpu.make_async_copy(pre_v.at[i], pre_out.at[i], sem_out.at[i])

    @pl.loop(0, 4)
    def _(i):
        pre_copy(i).start()

    @pl.loop(0, 4)
    def _(i):
        stored_copy(i).start()

    @pl.loop(0, 6)
    def _(j):
        weight_copy(j).start()

    barrier = pltpu.get_barrier_semaphore()

    def greet(dw, dn):
        pl.semaphore_signal(barrier, inc=1, device_id=(dw, dn), device_id_type=MESH)

    def b_device(t):
        return 4 * img + 2 * lax.div(t, 8) + core, lax.rem(t, 8)

    @pl.loop(1, 16)
    def _(k):
        greet(*b_device(lax.rem(me_b + k, 16)))
        greet(lax.rem(w + k, 16), n)

    @pl.loop(0, 8)
    def _(k):
        cw, cn = 4 * lax.div(k, 2) + grp, 2 * img + lax.rem(k, 2)

        @pl.when(jnp.logical_or(cw != w, cn != n))
        def _():
            greet(cw, cn)

        ew, en = 8 * core + k, lax.div(w, 2)

        @pl.when(jnp.logical_or(ew != w, en != n))
        def _():
            greet(ew, en)

    pl.semaphore_wait(barrier, 46 - c_self.astype(jnp.int32) - e_self.astype(jnp.int32))

    copy_a = pltpu.make_async_remote_copy(
        src_ref=part.at[1 - core],
        dst_ref=recv_a,
        send_sem=send_a.at[0],
        recv_sem=got_a.at[0],
        device_id=(w + 1 - 2 * core, n),
        device_id_type=MESH,
    )
    copy_a.start()

    eye = (
        lax.broadcasted_iota(jnp.int32, (64, 64), 0) == lax.broadcasted_iota(jnp.int32, (64, 64), 1)
    ).astype(F32).astype(BF16)
    at_ref[...] = dot_nt(eye, a_ref[...]).astype(BF16)

    def copy_b(src, slot, t, dev):
        return pltpu.make_async_remote_copy(
            src_ref=own.at[src],
            dst_ref=recv_b.at[slot],
            send_sem=send_b.at[t],
            recv_sem=got_b.at[slot],
            device_id=dev,
            device_id_type=MESH,
        )

    def start_b():
        own_copy.wait()
        copy_a.wait()

        @pl.loop(1, 17)
        def _(k):
            t = lax.rem(me_b + k, 16)
            own[t] = own[t] + recv_a[t]

            @pl.when(k < 16)
            def _():
                copy_b(t, me_b, t, b_device(t)).start()

    gates = gate_ref[...].astype(F32)
    scales = 1.0 + scale_ref[...].astype(F32)
    for i in range(4):
        gate_v[i] = jnp.broadcast_to(gates[i : i + 1], (8, D))
        scale_v[i] = jnp.broadcast_to(scales[i : i + 1], (8, D))

    @pl.loop(0, 4)
    def _(i):
        pre_copy(i).wait()

        @pl.loop(0, 16)
        def _(r):
            rows = pl.ds(pl.multiple_of(r * 16, 16), 16)
            here = pl.ds(pl.multiple_of(i * 256 + r * 16, 16), 16)
            for s in range(3):
                cols = slice(512 * s, 512 * s + 512)
                m = pre_v[i, rows, cols].astype(F32)
                sq = m * m
                h = 0.5 + 0.5 * jnp.tanh(m * (GELU_A + (GELU_A * 0.044715) * sq))
                val = m * h
                hid[here, cols] = val.astype(BF16)
                slope[here, cols] = h + (2.0 * val) * (1.0 - h) * (
                    GELU_A + (GELU_A * 0.134145) * sq
                )

        rows = pl.ds(pl.multiple_of(i * 256, 256), 256)
        lt = dot_nt(at_ref[...], hid[rows, :])
        low_part[2 * i] = lt[:, :128]
        low_part[2 * i + 1] = lt[:, 128:]

        @pl.when(i == 0)
        def _():
            start_b()

    def copy_l(t, slot):
        return pltpu.make_async_remote_copy(
            src_ref=low_part.at[t],
            dst_ref=recv_l.at[slot],
            send_sem=send_l.at[t],
            recv_sem=got_l.at[slot],
            device_id=(w, t),
            device_id_type=MESH,
        )

    @pl.loop(1, 8)
    def _(k):
        copy_l(lax.rem(n + k, 8), n).start()

    @pl.loop(0, 4)
    def _(i):
        stored_copy(i).wait()
        gate = gate_v[i, 0:1, :]
        scale = scale_v[i, 0:1, :]

        @pl.loop(0, 16)
        def _(r):
            rows = pl.ds(pl.multiple_of(r * 16, 16), 16)
            here = pl.ds(pl.multiple_of(i * 256 + r * 16, 16), 16)
            x = stored_v[i, rows, :].astype(F32)
            mean = jnp.sum(x, axis=1, keepdims=True) * (1.0 / D)
            x = x - mean
            var = jnp.sum(x * x, axis=1, keepdims=True) * (1.0 / D)
            zp[here, :] = (x * gate).astype(BF16)
            meanb[here, :] = jnp.broadcast_to(mean, (16, 128))
            invb[here, :] = jnp.broadcast_to(1.0 / jnp.sqrt(var + 1e-06), (16, 128))

        @pl.loop(0, 4)
        def _(r):
            rows = pl.ds(pl.multiple_of(r * 16, 16), 16)
            rows2 = pl.ds(pl.multiple_of(64 + r * 16, 16), 16)
            here = pl.ds(pl.multiple_of(1024 + 64 * i + r * 16, 16), 16)
            x = p_ref[rows, :].astype(F32) * scale
            x = x - jnp.sum(x, axis=1, keepdims=True) * (1.0 / D)
            xw[rows, :] = x.astype(BF16)
            zp[here, :] = (x * gate).astype(BF16)
            xw[rows2, :] = (u_ref[rows, :].astype(F32) * gate).astype(BF16)

        tokens = pl.ds(pl.multiple_of(i * 256, 256), 256)
        xs = xw[...]
        mean_row = jnp.transpose(meanb[tokens, :])[:1, :]
        sums = jnp.sum(xs.astype(F32), axis=1, keepdims=True)
        vbt[i] = dot_nt(xs, stored_v[i]) - sums * mean_row

    def copy_c(dn, slot):
        return pltpu.make_async_remote_copy(
            src_ref=red,
            dst_ref=recv_c.at[slot],
            send_sem=send_c.at[dn],
            recv_sem=got_c.at[slot],
            device_id=(c_wide, dn),
            device_id_type=MESH,
        )

    my_c_slot = 2 * img + lax.rem(n, 2)
    total = own[me_b]
    red[...] = total

    @pl.loop(1, 16)
    def _(k):
        t = lax.rem(me_b + k, 16)
        copy_b(t, t, t, b_device(t)).wait_recv()
        red[...] += recv_b[t]

    @pl.loop(1, 9)
    def _(k):
        dn = lax.rem(n + k, 8)

        @pl.when(jnp.logical_or(k < 8, jnp.logical_not(c_self)))
        def _():
            copy_c(dn, my_c_slot).start()

    @pl.when(c_self)
    def _():
        recv_c[my_c_slot] = red[...]

    def copy_m(t, slot):
        return pltpu.make_async_remote_copy(
            src_ref=red_l,
            dst_ref=recv_m.at[slot],
            send_sem=send_m.at[t],
            recv_sem=got_m.at[slot],
            device_id=(w, t),
            device_id_type=MESH,
        )

    red_l[...] = low_part[n]

    @pl.loop(1, 8)
    def _(k):
        t = lax.rem(n + k, 8)
        copy_l(t, t).wait_recv()
        red_l[...] += recv_l[t]

    recv_m[n] = red_l[...]

    @pl.loop(1, 8)
    def _(k):
        copy_m(lax.rem(n + k, 8), n).start()

    @pl.loop(0, 6)
    def _(j):
        weight_copy(j).wait()
        rows = pl.ds(pl.multiple_of(j * 256, 256), 256)
        nz[j] = dot_nt(zp[...], weight_v[rows, :])

    put = dot_nt(u_ref[...], zp[1024:1280, :])

    @pl.loop(0, 8)
    def _(k):
        sw, sn = 4 * lax.div(k, 2) + grp, 2 * img + lax.rem(k, 2)

        @pl.when(jnp.logical_or(sw != w, sn != n))
        def _():
            copy_c(0, k).wait_recv()

    @pl.loop(1, 8)
    def _(k):
        t = lax.rem(n + k, 8)
        copy_m(t, t).wait_recv()

    t1 = []
    for i in range(4):
        tok = slice(256 * i, 256 * i + 256)
        lat = jnp.concatenate([recv_c[2 * i], recv_c[2 * i + 1]], 1)
        pat = (lat * VAE_INVERSE).astype(BF16)
        pf = pat.astype(F32)
        inv = jnp.transpose(invb[tok, :])[:1, :]
        vb = vbt[i]
        k_row = inv * inv * (jnp.sum(pf * vb[:64], axis=0, keepdims=True) * (1.0 / D))
        pu = put[:, 64 * i : 64 * i + 64]
        pu_hi = pu.astype(BF16)
        pu_lo = (pu - pu_hi.astype(F32)).astype(BF16)
        back = (inv * (dot_nn(pu_hi, pat) + dot_nn(pu_lo, pat) - k_row * vb[64:])).astype(BF16)
        ip = inv * pf
        ip_hi = ip.astype(BF16)
        ip_lo = (ip - ip_hi.astype(F32)).astype(BF16)
        backt[:, tok] = back
        stack = jnp.concatenate([ip_hi, ip_lo, ip_hi, back], 0)
        ltile[tok, :] = jnp.transpose(stack.astype(F32)).astype(BF16)
        ik = inv * k_row
        ikcol[tok, :] = jnp.transpose(jnp.broadcast_to(ik, (128, 256)))
        low = (jnp.concatenate([recv_m[2 * i], recv_m[2 * i + 1]], 1) * NORM).astype(BF16)
        klt[:, tok] = (-ik * low.astype(F32)).astype(BF16)
        t1.append(dot_nt(low, ip_hi) + dot_nt(low, ip_lo))
    klt[:, 1024:1280] = jnp.concatenate(t1, 1).astype(BF16)

    up_t = dot_nn(klt[...], zp[:, pl.ds(pl.multiple_of(n * 384, 128), 384)])
    ubuf[0] = up_t[:, :256]
    ubuf[1] = pltpu.roll(up_t[:, 128:384], 192, 1)

    def copy_u(t, slot):
        return pltpu.make_async_remote_copy(
            src_ref=ubuf.at[lax.div(t, 8), pl.ds(pl.multiple_of(lax.rem(t, 8) * 8, 8), 8)],
            dst_ref=recv_u.at[slot],
            send_sem=send_u.at[t],
            recv_sem=got_u.at[slot],
            device_id=(t, n),
            device_id_type=MESH,
        )

    @pl.loop(1, 16)
    def _(k):
        copy_u(lax.rem(w + k, 16), w).start()

    down_t = dot_nn(backt[...], hid[...]) * NORM
    for t in range(16):
        first = 96 * t // 128 * 128
        off = 96 * t - first
        if off + 96 <= 128:
            piece = down_t[:, first : first + 128]
            piece = pltpu.roll(piece, 128 - off, 1) if off else piece
        else:
            piece = pltpu.roll(down_t[:, first : first + 256], 256 - off, 1)[:, :128]
        dbuf[t] = piece

    def copy_d(t, slot):
        return pltpu.make_async_remote_copy(
            src_ref=dbuf.at[t],
            dst_ref=recv_d.at[slot],
            send_sem=send_d.at[t],
            recv_sem=got_d.at[slot],
            device_id=(t, n),
            device_id_type=MESH,
        )

    @pl.loop(1, 16)
    def _(k):
        copy_d(lax.rem(w + k, 16), w).start()

    @pl.loop(0, 4)
    def _(i):
        rows = pl.ds(pl.multiple_of(i * 256, 256), 256)
        left = ltile[rows, :]
        coef = ikcol[rows, :]
        coef = jnp.concatenate([coef, coef], 1)
        for j in range(6):
            cols = slice(256 * j, 256 * j + 256)
            q = nz[j, pl.ds(pl.multiple_of(1024 + 64 * i, 64), 64), :]
            q_hi = q.astype(BF16)
            q_lo = (q - q_hi.astype(F32)).astype(BF16)
            right = jnp.concatenate([q_hi, q_hi, q_lo, at_ref[:, cols]], 0)
            grad = dot_nn(left, right) - coef * nz[j, rows, :]
            pre_v[i, :, cols] = (grad * slope[rows, cols]).astype(BF16)
        out_copy(i).start()

    def copy_e(dn, slot):
        return pltpu.make_async_remote_copy(
            src_ref=red_u,
            dst_ref=recv_e.at[slot],
            send_sem=send_e.at[dn],
            recv_sem=got_e.at[slot],
            device_id=(e_wide, dn),
            device_id_type=MESH,
        )

    my_e_slot = lax.rem(w, 8)
    red_u[...] = ubuf[lax.div(w, 8), pl.ds(pl.multiple_of(my_e_slot * 8, 8), 8)]

    @pl.loop(1, 16)
    def _(k):
        t = lax.rem(w + k, 16)
        copy_u(t, t).wait_recv()
        red_u[...] += recv_u[t]

    @pl.loop(1, 9)
    def _(k):
        dn = lax.rem(n + k, 8)

        @pl.when(jnp.logical_or(k < 8, jnp.logical_not(e_self)))
        def _():
            copy_e(dn, my_e_slot).start()

    @pl.when(e_self)
    def _():
        recv_e[my_e_slot] = red_u[...]

    recv_d[w] = dbuf[w]

    @pl.loop(1, 16)
    def _(k):
        t = lax.rem(w + k, 16)
        copy_d(t, t).wait_recv()

    down = recv_d[0]
    for t in range(1, 16):
        down = down + recv_d[t]
    down_out[...] = jnp.transpose(down)[:96, :]

    @pl.loop(0, 8)
    def _(k):
        @pl.when(jnp.logical_or(8 * core + k != w, lax.div(w, 2) != n))
        def _():
            copy_e(0, k).wait_recv()

    up = jnp.concatenate([recv_e[k] for k in range(8)], 0)
    up_out[...] = jnp.transpose(up)[:192, :]

    @pl.loop(1, 16)
    def _(k):
        t = lax.rem(me_b + k, 16)
        copy_b(t, t, t, b_device(t)).wait_send()
        t = lax.rem(w + k, 16)
        copy_u(t, t).wait_send()
        copy_d(t, t).wait_send()

    @pl.loop(1, 9)
    def _(k):
        dn = lax.rem(n + k, 8)

        @pl.when(k < 8)
        def _():
            copy_l(dn, n).wait_send()
            copy_m(dn, n).wait_send()

        @pl.when(jnp.logical_or(k < 8, jnp.logical_not(c_self)))
        def _():
            copy_c(dn, my_c_slot).wait_send()

        @pl.when(jnp.logical_or(k < 8, jnp.logical_not(e_self)))
        def _():
            copy_e(dn, my_e_slot).wait_send()

    @pl.loop(0, 4)
    def _(i):
        out_copy(i).wait()


def main(part, stored, pre, weight, a, u, p, scale, gate):
    dma = pltpu.SemaphoreType.DMA
    v = pltpu.VMEM
    anywhere = pl.BlockSpec(memory_space=pl.ANY)
    vmem = pl.BlockSpec(memory_space=pltpu.VMEM)
    return pl.pallas_call(
        main_kernel,
        out_shape=(
            jax.ShapeDtypeStruct((4, 256, F), BF16),
            jax.ShapeDtypeStruct((192, 64), F32),
            jax.ShapeDtypeStruct((96, 64), F32),
        ),
        in_specs=[anywhere] * 4 + [vmem] * 5,
        out_specs=(anywhere, vmem, vmem),
        scratch_shapes=[
            v((16, 64, 128), F32),
            v((16, 64, 128), F32),
            v((16, 64, 128), F32),
            v((64, 128), F32),
            v((8, 64, 128), F32),
            v((8, 64, 128), F32),
            v((8, 64, 128), F32),
            v((64, 128), F32),
            v((8, 64, 128), F32),
            v((2, 64, 256), F32),
            v((16, 8, 256), F32),
            v((8, 256), F32),
            v((8, 8, 256), F32),
            v((16, 64, 128), F32),
            v((16, 64, 128), F32),
            v((4, 256, D), BF16),
            v((4, 256, F), BF16),
            v((F, D), BF16),
            v((1280, D), BF16),
            v((128, D), BF16),
            v((1024, F), BF16),
            v((1024, F), F32),
            v((6, 1280, 256), F32),
            v((1024, 128), F32),
            v((1024, 128), F32),
            v((4, 128, 256), F32),
            v((1024, 128), F32),
            v((1024, 256), BF16),
            v((64, 1024), BF16),
            v((64, 1280), BF16),
            v((64, F), BF16),
            v((4, 8, D), F32),
            v((4, 8, D), F32),
            dma((1,)),
            dma((4,)),
            dma((4,)),
            dma((6,)),
            dma((4,)),
            dma((1,)),
            dma((1,)),
            dma((16,)),
            dma((16,)),
            dma((8,)),
            dma((8,)),
            dma((8,)),
            dma((8,)),
            dma((8,)),
            dma((8,)),
            dma((16,)),
            dma((16,)),
            dma((8,)),
            dma((8,)),
            dma((16,)),
            dma((16,)),
        ],
        compiler_params=pltpu.CompilerParams(
            collective_id=0, has_side_effects=True, vmem_limit_bytes=60 * MIB
        ),
        name="main",
    )(part, stored, pre, weight, a, u, p, scale, gate)


def local(
    cotangent,
    decoder_kernel,
    patch_projection_rows,
    stored_hidden_state,
    output_norm_scale,
    output_gate,
    preactivation_input,
    frozen_down_weight,
    adapter_down_rows,
    adapter_up_rows,
):
    offset = lax.axis_index("wide") % 4 * 128 + lax.axis_index("narrow") * 16
    kernel = lax.dynamic_slice_in_dim(decoder_kernel, offset, 16, 0).reshape(16, 144)
    part = conv(cotangent, kernel)
    return main(
        part,
        stored_hidden_state,
        preactivation_input,
        frozen_down_weight,
        adapter_down_rows,
        adapter_up_rows,
        patch_projection_rows,
        output_norm_scale,
        output_gate,
    )


def solution(mesh):
    placed = (
        P("wide", "narrow", None, None),
        P(),
        P(),
        P(None, "wide", None),
        P(),
        P(),
        P(None, "wide", "narrow"),
        P("narrow", None),
        P("narrow", None),
        P(),
    )
    return jax.shard_map(
        local,
        mesh=mesh,
        in_specs=placed,
        out_specs=(P(None, "wide", "narrow"), P("wide", None), P(("narrow", "wide"), None)),
        check_vma=False,
    )
```

time: 297 us -> 85.6 us (0.29)
  waiting for transfers between devices: 185 us -> 0 us
  Pallas kernels: 0 us -> 70.5 us
  matrix products: 55 us -> 0 us
  other arithmetic: 15.8 us -> 0 us
  between operations: 14.1 us -> 0.7 us
  starting transfers between devices: 11.3 us -> 0 us
    psum x1 -> x0, waiting for transfers between devices: 88 us -> none  [local(): latent = lax.psum(latent, 'narrow')]
    unnamed x5 -> x0, waiting for transfers between devices: 87.2 us -> none
    pallas_call x0 -> x2, Pallas kernels: none -> 70.5 us  [the longest x1 67.5 us: main(): pl.pallas_call(main_kernel, out_shape=(jax.ShapeDtypeStruct((4, 256, F),...]
    dot_general x16 -> x0, matrix products: 55 us -> none  [the longest x1 20.6 us: local(): jnp.einsum('bsd,fd->bsf', output_gradient, frozen_down_weight, preferred_...]
    all_to_all x1 -> x0, starting transfers between devices: 10.8 us -> none  [local(): lax.all_to_all(latent[None], 'wide', split_axis=2, concat_axis=0, tiled=T...]
    all_to_all x1 -> x0, waiting for transfers between devices: 9.77 us -> none  [local(): lax.all_to_all(latent[None], 'wide', split_axis=2, concat_axis=0, tiled=T...]
    reduce_sum x3 -> x0, other arithmetic: 8.32 us -> none  [the longest x1 4.55 us: local(): jnp.mean(centered * centered, axis=2, keepdims=True) + 1e-06]
    convert_element_type x3 -> x0, other arithmetic: 6.78 us -> none  [the longest x1 6.13 us: local(): (output_gate.astype(jnp.float32)[:, None, :] * inv_std * inner_term).asty...]
  transfers between devices with their start and end apart: 4 -> 0, of which waited for: 4 -> 0; matrix products, arithmetic and copies ran while one was open for 13% -> 0% of each run, Pallas kernels for 0% -> 0%
where the time goes in v1:
time: 85.6 us; the launch traced here: 85.2 us
  Pallas kernels  70.5 us (82%)
  local copies, waits for them, and re-layouts  14 us (16%)
    pallas_call x1, Pallas kernels, main(): pl.pallas_call(main_kernel, out_shape=(jax.ShapeDtypeStruct((4, 256, F),...  67.5 us
    unnamed x10, local copies, waits for them, and re-layouts  9.34 us
    pallas_call x2, local copies, waits for them, and re-layouts, main(): pl.pallas_call(main_kernel, out_shape=(jax.ShapeDtypeStruct((4, 256, F),...  3.1 us
    pallas_call x1, Pallas kernels, conv(): pl.pallas_call(conv_kernel, out_shape=jax.ShapeDtypeStruct((2, 16, 64, 12...  2.95 us

profile of v1, /device:TPU:1, one launch (start us, length us, event | category | flops | bytes accessed | tf_op | source)
XLA Modules:
  0.0 85.2 jit_solution(9007387161542508299)
XLA Ops:
  0.6 0.0 copy-start
  0.7 0.9 %copy-done = bf16[512,9,16]{0,2,1:T(8,128)(2,1)S(1)} copy-done((bf16[512,9,16]{0,2,1:T(8,128)(2,1)S(1)}, bf16[512,9,16]{0,2,1:T(8,128)(2,1)}, u32[]{:S(2)}) %copy-start) | copy-done | bytes 147480
  1.5 0.1 constant_dynamic-slice_fusion
  1.6 0.1 copy.21.k_ref
  1.7 1.9 %copy.22.a_ref = bf16[1536,64]{1,0:T(8,128)(2,1)} copy(bf16[1536,64]{0,1:T(8,128)(2,1)} %param.20) | data formatting | bytes 393216 | tf_op args[8]
  3.6 1.4 %copy.20 = bf16[128,16,128]{2,1,0:T(8,128)(2,1)S(1)} copy(bf16[128,16,128]{2,0,1:T(8,128)(2,1)} %bitcast.6) | data formatting | bytes 1048576 | tf_op jit(solution)/shard_map/transpose | solution.py:92
  5.0 0.0 copy-start.2
  5.0 1.0 %copy-done.2 = bf16[144,1024]{1,0:T(8,128)(2,1)S(1)} copy-done((bf16[144,1024]{1,0:T(8,128)(2,1)S(1)}, bf16[144,1024]{1,0:T(8,128)(2,1)}, u32[]{:S(2)}) %copy-start.2) | copy-done | bytes 294936
  5.9 0.0 copy-start.3
  5.9 0.9 %copy-done.3 = bf16[128,512]{1,0:T(8,128)(2,1)S(1)} copy-done((bf16[128,512]{1,0:T(8,128)(2,1)S(1)}, bf16[128,512]{1,0:T(8,128)(2,1)}, u32[]{:S(2)}) %copy-start.3) | copy-done | bytes 131096
  6.8 2.9 %conv.1.part = f32[2,16,64,128]{3,2,1,0:T(8,128)S(1)} custom-call(bf16[2048,128]{1,0:T(8,128)(2,1)S(1)} %bitcast.5, bf16[16,144]{1,0:T(8,128)(2,1)S(1)} %copy.21.k_ref, bf16[128,512]{1,0:T(8,128)(2,1)S(1)} %copy-done.3, bf16[144,1024]{1,0:T(8,128)(2,1)S(1)} %copy-done.2), custom_call_target="tpu_custom_call" | custom-call | tf_op jit(solution)/shard_map/conv/pallas_call | solution.py:93
  9.8 0.0 copy-start.1
  9.8 1.0 %copy-done.1 = f32[2,16,64,128]{3,2,1,0:T(8,128)} copy-done((f32[2,16,64,128]{3,2,1,0:T(8,128)}, f32[2,16,64,128]{3,2,1,0:T(8,128)S(1)}, u32[]{:S(2)}) %copy-start.1) | copy-done | bytes 1048600
  10.7 67.5 %main.1 = (bf16[4,256,1536]{2,1,0:T(8,128)(2,1)}, f32[192,64]{1,0:T(8,128)}, f32[96,64]{1,0:T(8,128)}) custom-call(f32[2,16,64,128]{3,2,1,0:T(8,128)} %copy-done.1, bf16[4,256,3072]{2,1,0:T(8,128)(2,1)} %stored.1, bf16[4,256,1536]{2,1,0:T(8,128)(2,1)} %pre.1, bf16[1536,3072]{1,0:T(8,128)(2,1)} %weight.1, bf16[1536,64]{1,0:T(8,128)(2,1)} %copy.22.a_ref, ...), custom_call_target="tpu_custom_call" | custom-call | tf_op jit(solution)/shard_map/main/pallas_call | solution.py:608
  78.3 1.5 %copy.24 = f32[96,64]{0,1:T(8,128)} copy(f32[96,64]{1,0:T(8,128)} %get-tuple-element.8) | data formatting | bytes 49152 | tf_op jit(solution)/shard_map/main/pallas_call | solution.py:608
  79.8 1.6 %copy.23 = f32[192,64]{0,1:T(8,128)} copy(f32[192,64]{1,0:T(8,128)} %get-tuple-element.7) | data formatting | bytes 98304 | tf_op jit(solution)/shard_map/main/pallas_call | solution.py:608
  81.4 3.8 %copy.26 = bf16[4,256,1536]{2,1,0:T(8,128)(2,1)} copy(bf16[4,256,1536]{2,1,0:T(8,128)(2,1)} %get-tuple-element.12) | data formatting | bytes 6291456
Async XLA Ops:
  0.6 0.9 %copy-start = (bf16[512,9,16]{0,2,1:T(8,128)(2,1)S(1)}, bf16[512,9,16]{0,2,1:T(8,128)(2,1)}, u32[]{:S(2)}) copy-start(bf16[512,9,16]{0,2,1:T(8,128)(2,1)} %param.13) | copy-start | bytes 442372
  5.0 1.0 %copy-start.2 = (bf16[144,1024]{1,0:T(8,128)(2,1)S(1)}, bf16[144,1024]{1,0:T(8,128)(2,1)}, u32[]{:S(2)}) copy-start(bf16[144,1024]{1,0:T(8,128)(2,1)} %constant.34.clone.sel_ref) | copy-start | bytes 884740
  5.9 0.9 %copy-start.3 = (bf16[128,512]{1,0:T(8,128)(2,1)S(1)}, bf16[128,512]{1,0:T(8,128)(2,1)}, u32[]{:S(2)}) copy-start(bf16[128,512]{1,0:T(8,128)(2,1)} %constant.33.clone.s_ref) | copy-start | bytes 393220
  9.8 1.0 %copy-start.1 = (f32[2,16,64,128]{3,2,1,0:T(8,128)}, f32[2,16,64,128]{3,2,1,0:T(8,128)S(1)}, u32[]{:S(2)}) copy-start(f32[2,16,64,128]{3,2,1,0:T(8,128)S(1)} %conv.1.part) | copy-start | bytes 3145732

commit v2 on v1

--- a/solution.py
+++ b/solution.py
@@ -1,8 +1,5 @@
-import functools
-
 import jax
 import jax.numpy as jnp
-import numpy as np
 from jax import lax
 from jax.experimental import pallas as pl
 from jax.experimental.pallas import tpu as pltpu
@@ -31,87 +28,44 @@
     return lax.dot_general(a, b, (((0,), (0,)), ((), ())), preferred_element_type=F32)
 
 
+def iota(shape, axis):
+    return lax.broadcasted_iota(jnp.int32, shape, axis)
+
+
+def one_hot(mask):
+    return mask.astype(F32).astype(BF16)
+
+
 def column_taps():
-    out = np.zeros((128, 512), np.float32)
-    for tap in range(4):
-        for q in range(64):
-            col = 2 * q - 1 + tap
-            if 0 <= col < 128:
-                out[col, 128 * tap + q] = 1
-                out[col, 128 * tap + 64 + q] = 1
-    return out
+    col = iota((128, 512), 1)
+    return one_hot(iota((128, 512), 0) == 2 * (col & 63) - 1 + (col >> 7))
 
 
 def kernel_taps():
-    out = np.zeros((144, 1024), np.float32)
-    for ty in range(4):
-        for tx in range(4):
-            for i in range(2):
-                for j in range(2):
-                    dy, dx = i + 2 - ty, j + 2 - tx
-                    if 0 <= dy < 3 and 0 <= dx < 3:
-                        for o in range(16):
-                            out[(3 * dy + dx) * 16 + o, (4 * ty + tx) * 64 + 4 * o + 2 * i + j] = 1
-    return out
-
-
-def conv_kernel(ft_ref, k_ref, s_ref, sel_ref, out_ref, g_ref, w_ref):
-    zero = jnp.zeros((16, 128), BF16)
-    for tap in range(4):
-        g_ref[tap, 0] = zero
-        g_ref[tap, 129] = zero
-
-    @pl.loop(0, 8)
-    def _(block):
-        rows = ft_ref[pl.ds(pl.multiple_of(block * 256, 256), 256), :]
-        for tap in range(4):
-            moved = dot_nn(rows, s_ref[:, 128 * tap : 128 * tap + 128])
-            g_ref[tap, pl.ds(1 + block * 16, 16)] = moved.astype(BF16).reshape(16, 16, 128)
-
-    taps = dot_nn(k_ref[...], sel_ref[...]).astype(BF16)
-    for t in range(16):
-        w_ref[16 * t : 16 * t + 16, :] = taps[:, 64 * t : 64 * t + 64]
-    weights = w_ref[...]
-    left = lax.broadcasted_iota(jnp.int32, (16, 128), 1) < 64
-
-    @pl.loop(0, 4)
-    def _(quarter):
-        for z in range(2):
-            for c in range(2):
-                for half in range(2):
-                    row = 32 * quarter + 16 * z + 8 * c + 4 * half
-                    window = [
-                        jnp.where(left, g_ref[tx, row + ty], g_ref[tx, row + 2 + ty])
-                        for ty in range(4)
-                        for tx in range(4)
-                    ]
-                    out_ref[c, 8 * z + 2 * quarter + half] = dot_tn(weights, jnp.concatenate(window, 0))
-
-
-def conv(cotangent, kernel):
-    ft = cotangent[0].transpose(1, 0, 2).reshape(2048, 128)
-    return pl.pallas_call(
-        conv_kernel,
-        out_shape=jax.ShapeDtypeStruct((2, 16, 64, 128), F32),
-        scratch_shapes=[pltpu.VMEM((4, 130, 16, 128), BF16), pltpu.VMEM((256, 64), BF16)],
-        compiler_params=pltpu.CompilerParams(vmem_limit_bytes=16 * MIB),
-        name="conv",
-    )(ft, kernel, jnp.asarray(column_taps(), BF16), jnp.asarray(kernel_taps(), BF16))
+    col = iota((16, 1024), 1)
+    same = iota((16, 1024), 0) == (col & 63) >> 2
+    dy = ((col >> 1) & 1) + 2 - (col >> 8)
+    dx = (col & 1) + 2 - ((col >> 6) & 3)
+    return jnp.concatenate(
+        [one_hot(same & (dy == t // 3) & (dx == t % 3)) for t in range(9)], 0
+    )
 
 
 def main_kernel(
-    part,
+    cot,
+    taps_in,
     stored,
     pre,
     weight,
-    a_ref,
-    u_ref,
-    p_ref,
-    scale_ref,
-    gate_ref,
+    a_in,
+    u_in,
+    p_in,
+    scale_in,
+    gate_in,
     pre_out,
     up_out,
     down_out,
+    give,
     own,
     recv_a,
     recv_b,
@@ -133,8 +87,15 @@
     zp,
     xw,
     hid,
-    slope,
     nz,
+    prod,
+    cot_v,
+    taps_v,
+    g_ref,
+    u_ref,
+    p_ref,
+    scale_ref,
+    gate_ref,
     meanb,
     invb,
     vbt,
@@ -178,8 +139,22 @@
     c_self = c_wide == w
     e_self = e_wide == w
 
-    own_copy = pltpu.make_async_copy(part.at[core], own, sem_local.at[0])
-    own_copy.start()
+    small = [
+        pltpu.make_async_copy(src, dst, sem_local.at[k])
+        for k, (src, dst) in enumerate(
+            [
+                (cot, cot_v),
+                (taps_in, taps_v),
+                (a_in, at_ref),
+                (gate_in, gate_ref),
+                (scale_in, scale_ref),
+                (p_in, p_ref),
+                (u_in, u_ref),
+            ]
+        )
+    ]
+    for copy in small:
+        copy.start()
 
     def pre_copy(i):
         return pltpu.make_async_copy(pre.at[i], pre_v.at[i], sem_pre.at[i])
@@ -233,10 +208,50 @@
         def _():
             greet(ew, en)
 
+    zero = jnp.zeros((16, 128), BF16)
+    for tap in range(4):
+        g_ref[tap, 0] = zero
+        g_ref[tap, 129] = zero
+    columns = column_taps()
+    routes = kernel_taps()
+    small[0].wait()
+
+    @pl.loop(0, 4)
+    def _(r):
+        rows = cot_v[:, pl.ds(pl.multiple_of(r * 32, 32), 32), :]
+        moved = dot_nn(jnp.swapaxes(rows, 0, 1).reshape(512, 128), columns)
+        for tap in range(4):
+            g_ref[tap, pl.ds(1 + r * 32, 32)] = (
+                moved[:, 128 * tap : 128 * tap + 128].astype(BF16).reshape(32, 16, 128)
+            )
+
+    small[1].wait()
+    pick = one_hot(iota((16, 512), 1) - grp * 128 - n * 16 == iota((16, 512), 0))
+    mine = dot_nn(dot_nt(pick, taps_v[...]).astype(BF16), routes)
+    mine = jnp.concatenate([mine[:, 64 * t : 64 * t + 64] for t in range(16)], 0)
+    weights = jnp.transpose(mine).astype(BF16)
+    left_half = iota((16, 128), 1) < 64
+
+    def conv(side, dst):
+        @pl.loop(0, 4)
+        def _(quarter):
+            for z in range(2):
+                for half in range(2):
+                    row = 32 * quarter + 16 * z + 8 * side + 4 * half
+                    window = [
+                        jnp.where(left_half, g_ref[tx, row + ty], g_ref[tx, row + 2 + ty])
+                        for ty in range(4)
+                        for tx in range(4)
+                    ]
+                    dst[8 * z + 2 * quarter + half] = dot_nn(
+                        weights, jnp.concatenate(window, 0)
+                    )
+
+    conv(1 - core, give)
     pl.semaphore_wait(barrier, 46 - c_self.astype(jnp.int32) - e_self.astype(jnp.int32))
 
     copy_a = pltpu.make_async_remote_copy(
-        src_ref=part.at[1 - core],
+        src_ref=give,
         dst_ref=recv_a,
         send_sem=send_a.at[0],
         recv_sem=got_a.at[0],
@@ -244,11 +259,9 @@
         device_id_type=MESH,
     )
     copy_a.start()
-
-    eye = (
-        lax.broadcasted_iota(jnp.int32, (64, 64), 0) == lax.broadcasted_iota(jnp.int32, (64, 64), 1)
-    ).astype(F32).astype(BF16)
-    at_ref[...] = dot_nt(eye, a_ref[...]).astype(BF16)
+    conv(core, own)
+    for copy in small[2:]:
+        copy.wait()
 
     def copy_b(src, slot, t, dev):
         return pltpu.make_async_remote_copy(
@@ -261,7 +274,6 @@
         )
 
     def start_b():
-        own_copy.wait()
         copy_a.wait()
 
         @pl.loop(1, 17)
@@ -292,11 +304,7 @@
                 m = pre_v[i, rows, cols].astype(F32)
                 sq = m * m
                 h = 0.5 + 0.5 * jnp.tanh(m * (GELU_A + (GELU_A * 0.044715) * sq))
-                val = m * h
-                hid[here, cols] = val.astype(BF16)
-                slope[here, cols] = h + (2.0 * val) * (1.0 - h) * (
-                    GELU_A + (GELU_A * 0.134145) * sq
-                )
+                hid[here, cols] = (m * h).astype(BF16)
 
         rows = pl.ds(pl.multiple_of(i * 256, 256), 256)
         lt = dot_nt(at_ref[...], hid[rows, :])
@@ -324,37 +332,53 @@
     @pl.loop(0, 4)
     def _(i):
         stored_copy(i).wait()
-        gate = gate_v[i, 0:1, :]
-        scale = scale_v[i, 0:1, :]
-
-        @pl.loop(0, 16)
+
+        @pl.loop(0, 16, unroll=4)
         def _(r):
-            rows = pl.ds(pl.multiple_of(r * 16, 16), 16)
             here = pl.ds(pl.multiple_of(i * 256 + r * 16, 16), 16)
-            x = stored_v[i, rows, :].astype(F32)
-            mean = jnp.sum(x, axis=1, keepdims=True) * (1.0 / D)
-            x = x - mean
-            var = jnp.sum(x * x, axis=1, keepdims=True) * (1.0 / D)
-            zp[here, :] = (x * gate).astype(BF16)
-            meanb[here, :] = jnp.broadcast_to(mean, (16, 128))
-            invb[here, :] = jnp.broadcast_to(1.0 / jnp.sqrt(var + 1e-06), (16, 128))
-
-        @pl.loop(0, 4)
+            acc = jnp.zeros((16, 128), F32)
+            for s in range(24):
+                cols = slice(128 * s, 128 * s + 128)
+                acc += stored_v[i, pl.ds(pl.multiple_of(r * 16, 16), 16), cols].astype(F32)
+            meanb[here, :] = acc
+
+        tokens = pl.ds(pl.multiple_of(i * 256, 256), 256)
+        mean = jnp.sum(meanb[tokens, :], axis=1, keepdims=True) * (1.0 / D)
+        meanb[tokens, :] = jnp.broadcast_to(mean, (256, 128))
+
+        @pl.loop(0, 16, unroll=4)
         def _(r):
-            rows = pl.ds(pl.multiple_of(r * 16, 16), 16)
-            rows2 = pl.ds(pl.multiple_of(64 + r * 16, 16), 16)
-            here = pl.ds(pl.multiple_of(1024 + 64 * i + r * 16, 16), 16)
-            x = p_ref[rows, :].astype(F32) * scale
-            x = x - jnp.sum(x, axis=1, keepdims=True) * (1.0 / D)
-            xw[rows, :] = x.astype(BF16)
-            zp[here, :] = (x * gate).astype(BF16)
-            xw[rows2, :] = (u_ref[rows, :].astype(F32) * gate).astype(BF16)
-
-        tokens = pl.ds(pl.multiple_of(i * 256, 256), 256)
-        xs = xw[...]
+            here = pl.ds(pl.multiple_of(i * 256 + r * 16, 16), 16)
+            mean = meanb[here, :]
+            acc = jnp.zeros((16, 128), F32)
+            for s in range(24):
+                cols = slice(128 * s, 128 * s + 128)
+                x = stored_v[i, pl.ds(pl.multiple_of(r * 16, 16), 16), cols].astype(F32) - mean
+                zp[here, cols] = (x * gate_v[i, 0:1, cols]).astype(BF16)
+                acc += x * x
+            invb[here, :] = acc
+
+        var = jnp.sum(invb[tokens, :], axis=1, keepdims=True) * (1.0 / D)
+        invb[tokens, :] = jnp.broadcast_to(1.0 / jnp.sqrt(var + 1e-06), (256, 128))
+
+        acc = jnp.zeros((64, 128), F32)
+        for s in range(24):
+            cols = slice(128 * s, 128 * s + 128)
+            acc += p_ref[:, cols].astype(F32) * scale_v[i, 0:1, cols]
+        mean = jnp.broadcast_to(jnp.sum(acc, axis=1, keepdims=True) * (1.0 / D), (64, 128))
+        acc = jnp.zeros((128, 128), F32)
+        here = pl.ds(pl.multiple_of(1024 + 64 * i, 64), 64)
+        for s in range(24):
+            cols = slice(128 * s, 128 * s + 128)
+            gate = gate_v[i, 0:1, cols]
+            x = p_ref[:, cols].astype(F32) * scale_v[i, 0:1, cols] - mean
+            zp[here, cols] = (x * gate).astype(BF16)
+            both = jnp.concatenate([x, u_ref[:, cols].astype(F32) * gate], 0).astype(BF16)
+            xw[:, cols] = both
+            acc += both.astype(F32)
+        sums = jnp.sum(acc, axis=1, keepdims=True)
         mean_row = jnp.transpose(meanb[tokens, :])[:1, :]
-        sums = jnp.sum(xs.astype(F32), axis=1, keepdims=True)
-        vbt[i] = dot_nt(xs, stored_v[i]) - sums * mean_row
+        vbt[i] = dot_nt(xw[...], stored_v[i]) - sums * mean_row
 
     def copy_c(dn, slot):
         return pltpu.make_async_remote_copy(
@@ -505,17 +529,22 @@
     @pl.loop(0, 4)
     def _(i):
         rows = pl.ds(pl.multiple_of(i * 256, 256), 256)
-        left = ltile[rows, :]
-        coef = ikcol[rows, :]
-        coef = jnp.concatenate([coef, coef], 1)
         for j in range(6):
             cols = slice(256 * j, 256 * j + 256)
             q = nz[j, pl.ds(pl.multiple_of(1024 + 64 * i, 64), 64), :]
             q_hi = q.astype(BF16)
             q_lo = (q - q_hi.astype(F32)).astype(BF16)
             right = jnp.concatenate([q_hi, q_hi, q_lo, at_ref[:, cols]], 0)
-            grad = dot_nn(left, right) - coef * nz[j, rows, :]
-            pre_v[i, :, cols] = (grad * slope[rows, cols]).astype(BF16)
+            prod[...] = dot_nn(ltile[rows, :], right)
+            for r in range(8):
+                here = pl.ds(pl.multiple_of(i * 256 + r * 32, 32), 32)
+                m = pre_v[i, 32 * r : 32 * r + 32, cols].astype(F32)
+                sq = m * m
+                h = 0.5 + 0.5 * jnp.tanh(m * (GELU_A + (GELU_A * 0.044715) * sq))
+                slope = h + (2.0 * m) * h * (1.0 - h) * (GELU_A + (GELU_A * 0.134145) * sq)
+                coef = ikcol[here, :]
+                grad = prod[32 * r : 32 * r + 32, :] - jnp.concatenate([coef, coef], 1) * nz[j, here, :]
+                pre_v[i, 32 * r : 32 * r + 32, cols] = (grad * slope).astype(BF16)
         out_copy(i).start()
 
     def copy_e(dn, slot):
@@ -559,7 +588,7 @@
     down = recv_d[0]
     for t in range(1, 16):
         down = down + recv_d[t]
-    down_out[...] = jnp.transpose(down)[:96, :]
+    down_out[...] = down[:, :96]
 
     @pl.loop(0, 8)
     def _(k):
@@ -568,7 +597,7 @@
             copy_e(0, k).wait_recv()
 
     up = jnp.concatenate([recv_e[k] for k in range(8)], 0)
-    up_out[...] = jnp.transpose(up)[:192, :]
+    up_out[...] = up[:, :192]
 
     @pl.loop(1, 16)
     def _(k):
@@ -600,7 +629,7 @@
         out_copy(i).wait()
 
 
-def main(part, stored, pre, weight, a, u, p, scale, gate):
+def main(*args):
     dma = pltpu.SemaphoreType.DMA
     v = pltpu.VMEM
     anywhere = pl.BlockSpec(memory_space=pl.ANY)
@@ -609,12 +638,13 @@
         main_kernel,
         out_shape=(
             jax.ShapeDtypeStruct((4, 256, F), BF16),
-            jax.ShapeDtypeStruct((192, 64), F32),
-            jax.ShapeDtypeStruct((96, 64), F32),
+            jax.ShapeDtypeStruct((64, 192), F32),
+            jax.ShapeDtypeStruct((64, 96), F32),
         ),
-        in_specs=[anywhere] * 4 + [vmem] * 5,
+        in_specs=[anywhere] * 10,
         out_specs=(anywhere, vmem, vmem),
         scratch_shapes=[
+            v((16, 64, 128), F32),
             v((16, 64, 128), F32),
             v((16, 64, 128), F32),
             v((16, 64, 128), F32),
@@ -636,8 +666,15 @@
             v((1280, D), BF16),
             v((128, D), BF16),
             v((1024, F), BF16),
-            v((1024, F), F32),
             v((6, 1280, 256), F32),
+            v((256, 256), F32),
+            v((16, 128, 128), BF16),
+            v((144, 512), BF16),
+            v((4, 130, 16, 128), BF16),
+            v((64, D), BF16),
+            v((64, D), BF16),
+            v((4, D), BF16),
+            v((4, D), BF16),
             v((1024, 128), F32),
             v((1024, 128), F32),
             v((4, 128, 256), F32),
@@ -648,7 +685,7 @@
             v((64, F), BF16),
             v((4, 8, D), F32),
             v((4, 8, D), F32),
-            dma((1,)),
+            dma((7,)),
             dma((4,)),
             dma((4,)),
             dma((6,)),
@@ -674,7 +711,7 @@
             collective_id=0, has_side_effects=True, vmem_limit_bytes=60 * MIB
         ),
         name="main",
-    )(part, stored, pre, weight, a, u, p, scale, gate)
+    )(*args)
 
 
 def local(
@@ -689,20 +726,19 @@
     adapter_down_rows,
     adapter_up_rows,
 ):
-    offset = lax.axis_index("wide") % 4 * 128 + lax.axis_index("narrow") * 16
-    kernel = lax.dynamic_slice_in_dim(decoder_kernel, offset, 16, 0).reshape(16, 144)
-    part = conv(cotangent, kernel)
-    return main(
-        part,
+    pre_grad, up_grad, down_grad = main(
+        cotangent[0],
+        decoder_kernel.transpose(1, 2, 0).reshape(144, 512),
         stored_hidden_state,
         preactivation_input,
         frozen_down_weight,
-        adapter_down_rows,
+        adapter_down_rows.T,
         adapter_up_rows,
         patch_projection_rows,
         output_norm_scale,
         output_gate,
     )
+    return pre_grad, up_grad.T, down_grad.T
 
 
 def solution(mesh):

time: 85.6 us -> 59.8 us (0.70)
  Pallas kernels: 70.5 us -> 53.9 us
  local copies, waits for them, and re-layouts: 14 us -> 5.04 us
    pallas_call x1, Pallas kernels: 67.5 us -> 53.9 us  [main(): pl.pallas_call(main_kernel, out_shape=(jax.ShapeDtypeStruct((4, 256, F),...]
    unnamed x10 -> x7, local copies, waits for them, and re-layouts: 9.34 us -> 5.04 us
    pallas_call x2 -> x0, local copies, waits for them, and re-layouts: 3.1 us -> none  [main(): pl.pallas_call(main_kernel, out_shape=(jax.ShapeDtypeStruct((4, 256, F),...]
    pallas_call x1 -> x0, Pallas kernels: 2.95 us -> none  [conv(): pl.pallas_call(conv_kernel, out_shape=jax.ShapeDtypeStruct((2, 16, 64, 12...]
    transpose x1 -> x0, local copies, waits for them, and re-layouts: 1.38 us -> none  [conv(): ft = cotangent[0].transpose(1, 0, 2).reshape(2048, 128)]
where the time goes in v2:
time: 59.8 us; the launch traced here: 59.6 us
  Pallas kernels  53.9 us (90%)
  local copies, waits for them, and re-layouts  5.04 us (8%)
  between operations  0.66 us (1%)
    pallas_call x1, Pallas kernels, main(): pl.pallas_call(main_kernel, out_shape=(jax.ShapeDtypeStruct((4, 256, F),...  53.9 us
    unnamed x7, local copies, waits for them, and re-layouts  5.04 us

profile of v2, /device:TPU:1, one launch (start us, length us, event | category | flops | bytes accessed | tf_op | source)
XLA Modules:
  0.0 59.6 jit_solution(7066963862930211514)
XLA Ops:
  0.6 53.9 %main.1 = (bf16[4,256,1536]{2,1,0:T(8,128)(2,1)}, f32[64,192]{1,0:T(8,128)}, f32[64,96]{1,0:T(8,128)}) custom-call(bf16[16,128,128]{2,1,0:T(8,128)(2,1)} %bitcast.7, bf16[144,512]{1,0:T(8,128)(2,1)} %bitcast.9, bf16[4,256,3072]{2,1,0:T(8,128)(2,1)} %stored.1, bf16[4,256,1536]{2,1,0:T(8,128)(2,1)} %pre.1, bf16[1536,3072]{1,0:T(8,128)(2,1)} %weight.1, ...), custom_call_target="tpu_custom_call" | custom-call | tf_op jit(solution)/shard_map/main/pallas_call | solution.py:637
  54.6 0.0 copy-start
  54.6 0.0 copy-start.1
  54.6 3.8 %copy.16 = bf16[4,256,1536]{2,1,0:T(8,128)(2,1)} copy(bf16[4,256,1536]{2,1,0:T(8,128)(2,1)} %get-tuple-element.12) | data formatting | bytes 6291456
  58.4 0.0 copy-done
  58.4 0.6 %copy.17 = f32[192,64]{0,1:T(8,128)} copy(f32[192,64]{0,1:T(8,128)S(1)} %bitcast.10) | data formatting | bytes 98304
  59.0 0.0 copy-done.1
  59.0 0.6 %copy.18 = f32[96,64]{0,1:T(8,128)} copy(f32[96,64]{0,1:T(8,128)S(1)} %bitcast.11) | data formatting | bytes 49152
Async XLA Ops:
  54.6 3.8 %copy-start = (f32[64,192]{1,0:T(8,128)S(1)}, f32[64,192]{1,0:T(8,128)}, u32[]{:S(2)}) copy-start(f32[64,192]{1,0:T(8,128)} %get-tuple-element.7) | copy-start | bytes 147460
  54.6 4.4 %copy-start.1 = (f32[64,96]{1,0:T(8,128)S(1)}, f32[64,96]{1,0:T(8,128)}, u32[]{:S(2)}) copy-start(f32[64,96]{1,0:T(8,128)} %get-tuple-element.8) | copy-start | bytes 73732

commit v3 on v2

--- a/solution.py
+++ b/solution.py
@@ -65,7 +65,6 @@
     pre_out,
     up_out,
     down_out,
-    give,
     own,
     recv_a,
     recv_b,
@@ -84,11 +83,18 @@
     stored_v,
     pre_v,
     weight_v,
-    zp,
-    xw,
+    z0,
+    z1,
+    z2,
+    z3,
+    pc,
+    xw0,
+    xw1,
     hid,
+    slope,
     nz,
-    prod,
+    prod0,
+    prod1,
     cot_v,
     taps_v,
     g_ref,
@@ -128,6 +134,9 @@
     send_d,
     got_d,
 ):
+    zps = (z0, z1, z2, z3)
+    xws = (xw0, xw1)
+    prods = (prod0, prod1)
     w = lax.axis_index("wide")
     n = lax.axis_index("narrow")
     img = lax.div(w, 4)
@@ -169,17 +178,20 @@
     def out_copy(i):
         return pltpu.make_async_copy(pre_v.at[i], pre_out.at[i], sem_out.at[i])
 
+    stored_copy(0).start()
+
+    @pl.loop(0, 6)
+    def _(j):
+        weight_copy(j).start()
+
+    stored_copy(1).start()
+
     @pl.loop(0, 4)
     def _(i):
         pre_copy(i).start()
 
-    @pl.loop(0, 4)
-    def _(i):
-        stored_copy(i).start()
-
-    @pl.loop(0, 6)
-    def _(j):
-        weight_copy(j).start()
+    stored_copy(2).start()
+    stored_copy(3).start()
 
     barrier = pltpu.get_barrier_semaphore()
 
@@ -247,11 +259,11 @@
                         weights, jnp.concatenate(window, 0)
                     )
 
-    conv(1 - core, give)
+    conv(1 - core, dbuf)
     pl.semaphore_wait(barrier, 46 - c_self.astype(jnp.int32) - e_self.astype(jnp.int32))
 
     copy_a = pltpu.make_async_remote_copy(
-        src_ref=give,
+        src_ref=dbuf,
         dst_ref=recv_a,
         send_sem=send_a.at[0],
         recv_sem=got_a.at[0],
@@ -291,29 +303,91 @@
         gate_v[i] = jnp.broadcast_to(gates[i : i + 1], (8, D))
         scale_v[i] = jnp.broadcast_to(scales[i : i + 1], (8, D))
 
-    @pl.loop(0, 4)
-    def _(i):
-        pre_copy(i).wait()
-
-        @pl.loop(0, 16)
+    def stats(i):
+        @pl.loop(0, 16, unroll=16)
         def _(r):
-            rows = pl.ds(pl.multiple_of(r * 16, 16), 16)
-            here = pl.ds(pl.multiple_of(i * 256 + r * 16, 16), 16)
+            acc = jnp.zeros((16, 128), F32)
+            for s in range(24):
+                cols = slice(128 * s, 128 * s + 128)
+                acc += stored_v[i, pl.ds(r * 16, 16), cols].astype(F32)
+            meanb[pl.ds(i * 256 + r * 16, 16), :] = acc
+
+        tokens = slice(256 * i, 256 * i + 256)
+        mean = jnp.sum(meanb[tokens, :], axis=1, keepdims=True) * (1.0 / D)
+        meanb[tokens, :] = jnp.broadcast_to(mean, (256, 128))
+
+        @pl.loop(0, 16, unroll=16)
+        def _(r):
+            here = pl.ds(i * 256 + r * 16, 16)
+            mean = meanb[here, :]
+            acc = jnp.zeros((16, 128), F32)
+            for s in range(24):
+                cols = slice(128 * s, 128 * s + 128)
+                x = stored_v[i, pl.ds(r * 16, 16), cols].astype(F32) - mean
+                zps[i][pl.ds(r * 16, 16), cols] = (x * gate_v[i, 0:1, cols]).astype(BF16)
+                acc += x * x
+            invb[here, :] = acc
+
+        var = jnp.sum(invb[tokens, :], axis=1, keepdims=True) * (1.0 / D)
+        invb[tokens, :] = jnp.broadcast_to(1.0 / jnp.sqrt(var + 1e-06), (256, 128))
+
+    def prep(i):
+        def total(s, acc):
+            cols = pl.ds(128 * s, 128)
+            return acc + p_ref[:, cols].astype(F32) * scale_v[i, 0:1, cols]
+
+        acc = lax.fori_loop(0, 24, total, jnp.zeros((64, 128), F32), unroll=24)
+        mean = jnp.broadcast_to(jnp.sum(acc, axis=1, keepdims=True) * (1.0 / D), (64, 128))
+
+        def fill(s, acc):
+            cols = pl.ds(128 * s, 128)
+            gate = gate_v[i, 0:1, cols]
+            x = p_ref[:, cols].astype(F32) * scale_v[i, 0:1, cols] - mean
+            pc[64 * i : 64 * i + 64, cols] = (x * gate).astype(BF16)
+            both = jnp.concatenate([x, u_ref[:, cols].astype(F32) * gate], 0).astype(BF16)
+            xws[i % 2][:, cols] = both
+            return acc + both.astype(F32)
+
+        acc = lax.fori_loop(0, 24, fill, jnp.zeros((128, 128), F32), unroll=24)
+        return jnp.sum(acc, axis=1, keepdims=True)
+
+    def large(i):
+        nz[256 * i : 256 * i + 256, :] = dot_nt(zps[i][...], weight_v[...])
+
+    def small_products(i, sums):
+        tokens = slice(256 * i, 256 * i + 256)
+        mean_row = jnp.transpose(meanb[tokens, :])[:1, :]
+        vbt[i] = dot_nt(xws[i % 2][...], stored_v[i]) - sums * mean_row
+
+    def gelu(i):
+        @pl.loop(0, 16, unroll=16)
+        def _(r):
+            rows = pl.ds(r * 16, 16)
+            here = pl.ds(i * 256 + r * 16, 16)
+            for s in range(3):
+                cols = slice(512 * s, 512 * s + 512)
+                m = pre_v[i, rows, cols].astype(F32)
+                h = 0.5 + 0.5 * jnp.tanh(m * (GELU_A + (GELU_A * 0.044715) * (m * m)))
+                hid[here, cols] = (m * h).astype(BF16)
+
+    def slopes(i):
+        @pl.loop(0, 16, unroll=16)
+        def _(r):
+            rows = pl.ds(r * 16, 16)
+            here = pl.ds(i * 256 + r * 16, 16)
             for s in range(3):
                 cols = slice(512 * s, 512 * s + 512)
                 m = pre_v[i, rows, cols].astype(F32)
                 sq = m * m
                 h = 0.5 + 0.5 * jnp.tanh(m * (GELU_A + (GELU_A * 0.044715) * sq))
-                hid[here, cols] = (m * h).astype(BF16)
-
-        rows = pl.ds(pl.multiple_of(i * 256, 256), 256)
-        lt = dot_nt(at_ref[...], hid[rows, :])
-        low_part[2 * i] = lt[:, :128]
-        low_part[2 * i + 1] = lt[:, 128:]
-
-        @pl.when(i == 0)
-        def _():
-            start_b()
+                slope[here, cols] = h + (2.0 * m) * h * (1.0 - h) * (
+                    GELU_A + (GELU_A * 0.134145) * sq
+                )
+
+    stored_copy(0).wait()
+    sums = prep(0)
+    stats(0)
+    start_b()
 
     def copy_l(t, slot):
         return pltpu.make_async_remote_copy(
@@ -325,60 +399,33 @@
             device_id_type=MESH,
         )
 
+    @pl.loop(0, 6)
+    def _(j):
+        weight_copy(j).wait()
+
+    stored_copy(1).wait()
+    for i in range(4):
+        pre_copy(i).wait()
+    large(0)
+    small_products(0, sums)
+    stats(1)
+    sums = prep(1)
+    for i in range(4):
+        gelu(i)
+    for i in range(4):
+        lt = dot_nt(at_ref[...], hid[256 * i : 256 * i + 256, :])
+        low_part[2 * i] = lt[:, :128]
+        low_part[2 * i + 1] = lt[:, 128:]
+
     @pl.loop(1, 8)
     def _(k):
         copy_l(lax.rem(n + k, 8), n).start()
 
-    @pl.loop(0, 4)
-    def _(i):
-        stored_copy(i).wait()
-
-        @pl.loop(0, 16, unroll=4)
-        def _(r):
-            here = pl.ds(pl.multiple_of(i * 256 + r * 16, 16), 16)
-            acc = jnp.zeros((16, 128), F32)
-            for s in range(24):
-                cols = slice(128 * s, 128 * s + 128)
-                acc += stored_v[i, pl.ds(pl.multiple_of(r * 16, 16), 16), cols].astype(F32)
-            meanb[here, :] = acc
-
-        tokens = pl.ds(pl.multiple_of(i * 256, 256), 256)
-        mean = jnp.sum(meanb[tokens, :], axis=1, keepdims=True) * (1.0 / D)
-        meanb[tokens, :] = jnp.broadcast_to(mean, (256, 128))
-
-        @pl.loop(0, 16, unroll=4)
-        def _(r):
-            here = pl.ds(pl.multiple_of(i * 256 + r * 16, 16), 16)
-            mean = meanb[here, :]
-            acc = jnp.zeros((16, 128), F32)
-            for s in range(24):
-                cols = slice(128 * s, 128 * s + 128)
-                x = stored_v[i, pl.ds(pl.multiple_of(r * 16, 16), 16), cols].astype(F32) - mean
-                zp[here, cols] = (x * gate_v[i, 0:1, cols]).astype(BF16)
-                acc += x * x
-            invb[here, :] = acc
-
-        var = jnp.sum(invb[tokens, :], axis=1, keepdims=True) * (1.0 / D)
-        invb[tokens, :] = jnp.broadcast_to(1.0 / jnp.sqrt(var + 1e-06), (256, 128))
-
-        acc = jnp.zeros((64, 128), F32)
-        for s in range(24):
-            cols = slice(128 * s, 128 * s + 128)
-            acc += p_ref[:, cols].astype(F32) * scale_v[i, 0:1, cols]
-        mean = jnp.broadcast_to(jnp.sum(acc, axis=1, keepdims=True) * (1.0 / D), (64, 128))
-        acc = jnp.zeros((128, 128), F32)
-        here = pl.ds(pl.multiple_of(1024 + 64 * i, 64), 64)
-        for s in range(24):
-            cols = slice(128 * s, 128 * s + 128)
-            gate = gate_v[i, 0:1, cols]
-            x = p_ref[:, cols].astype(F32) * scale_v[i, 0:1, cols] - mean
-            zp[here, cols] = (x * gate).astype(BF16)
-            both = jnp.concatenate([x, u_ref[:, cols].astype(F32) * gate], 0).astype(BF16)
-            xw[:, cols] = both
-            acc += both.astype(F32)
-        sums = jnp.sum(acc, axis=1, keepdims=True)
-        mean_row = jnp.transpose(meanb[tokens, :])[:1, :]
-        vbt[i] = dot_nt(xw[...], stored_v[i]) - sums * mean_row
+    stored_copy(2).wait()
+    large(1)
+    small_products(1, sums)
+    stats(2)
+    sums = prep(2)
 
     def copy_c(dn, slot):
         return pltpu.make_async_remote_copy(
@@ -436,13 +483,15 @@
     def _(k):
         copy_m(lax.rem(n + k, 8), n).start()
 
-    @pl.loop(0, 6)
-    def _(j):
-        weight_copy(j).wait()
-        rows = pl.ds(pl.multiple_of(j * 256, 256), 256)
-        nz[j] = dot_nt(zp[...], weight_v[rows, :])
-
-    put = dot_nt(u_ref[...], zp[1024:1280, :])
+    stored_copy(3).wait()
+    large(2)
+    small_products(2, sums)
+    stats(3)
+    sums = prep(3)
+    slopes(0)
+    slopes(1)
+    small_products(3, sums)
+    put = dot_nt(u_ref[...], pc[...])
 
     @pl.loop(0, 8)
     def _(k):
@@ -483,7 +532,10 @@
         t1.append(dot_nt(low, ip_hi) + dot_nt(low, ip_lo))
     klt[:, 1024:1280] = jnp.concatenate(t1, 1).astype(BF16)
 
-    up_t = dot_nn(klt[...], zp[:, pl.ds(pl.multiple_of(n * 384, 128), 384)])
+    mine = pl.ds(pl.multiple_of(n * 384, 128), 384)
+    up_t = dot_nn(klt[:, 1024:1280], pc[:, mine])
+    for i in range(4):
+        up_t += dot_nn(klt[:, 256 * i : 256 * i + 256], zps[i][:, mine])
     ubuf[0] = up_t[:, :256]
     ubuf[1] = pltpu.roll(up_t[:, 128:384], 192, 1)
 
@@ -526,26 +578,9 @@
     def _(k):
         copy_d(lax.rem(w + k, 16), w).start()
 
-    @pl.loop(0, 4)
-    def _(i):
-        rows = pl.ds(pl.multiple_of(i * 256, 256), 256)
-        for j in range(6):
-            cols = slice(256 * j, 256 * j + 256)
-            q = nz[j, pl.ds(pl.multiple_of(1024 + 64 * i, 64), 64), :]
-            q_hi = q.astype(BF16)
-            q_lo = (q - q_hi.astype(F32)).astype(BF16)
-            right = jnp.concatenate([q_hi, q_hi, q_lo, at_ref[:, cols]], 0)
-            prod[...] = dot_nn(ltile[rows, :], right)
-            for r in range(8):
-                here = pl.ds(pl.multiple_of(i * 256 + r * 32, 32), 32)
-                m = pre_v[i, 32 * r : 32 * r + 32, cols].astype(F32)
-                sq = m * m
-                h = 0.5 + 0.5 * jnp.tanh(m * (GELU_A + (GELU_A * 0.044715) * sq))
-                slope = h + (2.0 * m) * h * (1.0 - h) * (GELU_A + (GELU_A * 0.134145) * sq)
-                coef = ikcol[here, :]
-                grad = prod[32 * r : 32 * r + 32, :] - jnp.concatenate([coef, coef], 1) * nz[j, here, :]
-                pre_v[i, 32 * r : 32 * r + 32, cols] = (grad * slope).astype(BF16)
-        out_copy(i).start()
+    large(3)
+    slopes(2)
+    slopes(3)
 
     def copy_e(dn, slot):
         return pltpu.make_async_remote_copy(
@@ -577,6 +612,37 @@
     @pl.when(e_self)
     def _():
         recv_e[my_e_slot] = red_u[...]
+
+    nz[1024:1280, :] = dot_nt(pc[...], weight_v[...])
+
+    def grads(i, h):
+        cols = slice(768 * h, 768 * h + 768)
+        q = nz[1024 + 64 * i : 1088 + 64 * i, cols]
+        q_hi = q.astype(BF16)
+        q_lo = (q - q_hi.astype(F32)).astype(BF16)
+        right = jnp.concatenate([q_hi, q_hi, q_lo, at_ref[:, cols]], 0)
+        prods[h][...] = dot_nn(ltile[256 * i : 256 * i + 256, :], right)
+
+    def finish(i, h):
+        @pl.loop(0, 16, unroll=16)
+        def _(r):
+            rows = pl.ds(r * 16, 16)
+            here = pl.ds(i * 256 + r * 16, 16)
+            coef = ikcol[here, :]
+            coef = jnp.concatenate([coef] * 3, 1)
+            for s in range(2):
+                cols = slice(768 * h + 384 * s, 768 * h + 384 * s + 384)
+                grad = prods[h][rows, 384 * s : 384 * s + 384] - coef * nz[here, cols]
+                pre_v[i, rows, cols] = (grad * slope[here, cols]).astype(BF16)
+
+    grads(0, 0)
+    for i in range(4):
+        grads(i, 1)
+        finish(i, 0)
+        if i < 3:
+            grads(i + 1, 0)
+        finish(i, 1)
+        out_copy(i).start()
 
     recv_d[w] = dbuf[w]
 
@@ -647,7 +713,6 @@
             v((16, 64, 128), F32),
             v((16, 64, 128), F32),
             v((16, 64, 128), F32),
-            v((16, 64, 128), F32),
             v((64, 128), F32),
             v((8, 64, 128), F32),
             v((8, 64, 128), F32),
@@ -663,11 +728,18 @@
             v((4, 256, D), BF16),
             v((4, 256, F), BF16),
             v((F, D), BF16),
-            v((1280, D), BF16),
+            v((256, D), BF16),
+            v((256, D), BF16),
+            v((256, D), BF16),
+            v((256, D), BF16),
+            v((256, D), BF16),
+            v((128, D), BF16),
             v((128, D), BF16),
             v((1024, F), BF16),
-            v((6, 1280, 256), F32),
-            v((256, 256), F32),
+            v((1024, F), F32),
+            v((1280, F), F32),
+            v((256, F // 2), F32),
+            v((256, F // 2), F32),
             v((16, 128, 128), BF16),
             v((144, 512), BF16),
             v((4, 130, 16, 128), BF16),
@@ -708,7 +780,7 @@
             dma((16,)),
         ],
         compiler_params=pltpu.CompilerParams(
-            collective_id=0, has_side_effects=True, vmem_limit_bytes=60 * MIB
+            collective_id=0, has_side_effects=True, vmem_limit_bytes=62 * MIB
         ),
         name="main",
     )(*args)

time: 59.8 us -> 55.3 us (0.925)
  Pallas kernels: 53.9 us -> 49.2 us
    pallas_call x1, Pallas kernels: 53.9 us -> 49.2 us  [main(): pl.pallas_call(main_kernel, out_shape=(jax.ShapeDtypeStruct((4, 256, F),...]
where the time goes in v3:
time: 55.3 us; the launch traced here: 54.9 us
  Pallas kernels  49.2 us (89%)
  local copies, waits for them, and re-layouts  5.04 us (9%)
  between operations  0.66 us (1%)
    pallas_call x1, Pallas kernels, main(): pl.pallas_call(main_kernel, out_shape=(jax.ShapeDtypeStruct((4, 256, F),...  49.2 us
    unnamed x7, local copies, waits for them, and re-layouts  5.04 us

profile of v3, /device:TPU:1, one launch (start us, length us, event | category | flops | bytes accessed | tf_op | source)
XLA Modules:
  0.0 54.9 jit_solution(18019636870197811848)
XLA Ops:
  0.6 49.2 %main.1 = (bf16[4,256,1536]{2,1,0:T(8,128)(2,1)}, f32[64,192]{1,0:T(8,128)}, f32[64,96]{1,0:T(8,128)}) custom-call(bf16[16,128,128]{2,1,0:T(8,128)(2,1)} %bitcast.7, bf16[144,512]{1,0:T(8,128)(2,1)} %bitcast.9, bf16[4,256,3072]{2,1,0:T(8,128)(2,1)} %stored.1, bf16[4,256,1536]{2,1,0:T(8,128)(2,1)} %pre.1, bf16[1536,3072]{1,0:T(8,128)(2,1)} %weight.1, ...), custom_call_target="tpu_custom_call" | custom-call | tf_op jit(solution)/shard_map/main/pallas_call | solution.py:703
  49.9 0.0 copy-start
  49.9 0.0 copy-start.1
  49.9 3.8 %copy.16 = bf16[4,256,1536]{2,1,0:T(8,128)(2,1)} copy(bf16[4,256,1536]{2,1,0:T(8,128)(2,1)} %get-tuple-element.12) | data formatting | bytes 6291456
  53.7 0.0 copy-done
  53.7 0.6 %copy.17 = f32[192,64]{0,1:T(8,128)} copy(f32[192,64]{0,1:T(8,128)S(1)} %bitcast.10) | data formatting | bytes 98304
  54.3 0.0 copy-done.1
  54.3 0.6 %copy.18 = f32[96,64]{0,1:T(8,128)} copy(f32[96,64]{0,1:T(8,128)S(1)} %bitcast.11) | data formatting | bytes 49152
Async XLA Ops:
  49.9 3.8 %copy-start = (f32[64,192]{1,0:T(8,128)S(1)}, f32[64,192]{1,0:T(8,128)}, u32[]{:S(2)}) copy-start(f32[64,192]{1,0:T(8,128)} %get-tuple-element.7) | copy-start | bytes 147460
  49.9 4.4 %copy-start.1 = (f32[64,96]{1,0:T(8,128)S(1)}, f32[64,96]{1,0:T(8,128)}, u32[]{:S(2)}) copy-start(f32[64,96]{1,0:T(8,128)} %get-tuple-element.8) | copy-start | bytes 73732

commit v4 on v3

--- a/solution.py
+++ b/solution.py
@@ -226,21 +226,19 @@
         g_ref[tap, 129] = zero
     columns = column_taps()
     routes = kernel_taps()
+    pick = one_hot(iota((16, 512), 1) - grp * 128 - n * 16 == iota((16, 512), 0))
     small[0].wait()
-
-    @pl.loop(0, 4)
-    def _(r):
-        rows = cot_v[:, pl.ds(pl.multiple_of(r * 32, 32), 32), :]
-        moved = dot_nn(jnp.swapaxes(rows, 0, 1).reshape(512, 128), columns)
-        for tap in range(4):
-            g_ref[tap, pl.ds(1 + r * 32, 32)] = (
-                moved[:, 128 * tap : 128 * tap + 128].astype(BF16).reshape(32, 16, 128)
-            )
-
     small[1].wait()
-    pick = one_hot(iota((16, 512), 1) - grp * 128 - n * 16 == iota((16, 512), 0))
     mine = dot_nn(dot_nt(pick, taps_v[...]).astype(BF16), routes)
     mine = jnp.concatenate([mine[:, 64 * t : 64 * t + 64] for t in range(16)], 0)
+    for r in range(4):
+        rows = jnp.swapaxes(cot_v[:, 32 * r : 32 * r + 32, :], 0, 1).reshape(512, 128)
+        moved = dot_nn(rows, columns).astype(BF16)
+        for tap in range(4):
+            g_ref[tap, 1 + 32 * r : 33 + 32 * r] = moved[:, 128 * tap : 128 * tap + 128].reshape(
+                32, 16, 128
+            )
+
     weights = jnp.transpose(mine).astype(BF16)
     left_half = iota((16, 128), 1) < 64
 
@@ -786,6 +784,43 @@
     )(*args)
 
 
+def place_kernel(pre, up, down, pre_out, up_out, down_out, pre_v, up_v, down_v, sem_in, sem_out):
+    pieces = [
+        (pre.at[i, rows], pre_v.at[i, rows], pre_out.at[i, rows])
+        for i in range(4)
+        for rows in (pl.ds(0, 128), pl.ds(128, 128))
+    ]
+    pieces += [(up, up_v, up_out), (down, down_v, down_out)]
+    into = [
+        pltpu.make_async_copy(src, mid, sem_in.at[k]) for k, (src, mid, _) in enumerate(pieces)
+    ]
+    out = [
+        pltpu.make_async_copy(mid, dst, sem_out.at[k]) for k, (_, mid, dst) in enumerate(pieces)
+    ]
+    for copy in into:
+        copy.start()
+    for first, second in zip(into, out):
+        first.wait()
+        second.start()
+    for copy in out:
+        copy.wait()
+
+
+def place(*arrays):
+    shapes = [(a.shape, a.dtype) for a in arrays]
+    anywhere = pl.BlockSpec(memory_space=pl.ANY)
+    return pl.pallas_call(
+        place_kernel,
+        out_shape=tuple(jax.ShapeDtypeStruct(*s) for s in shapes),
+        in_specs=[anywhere] * 3,
+        out_specs=(anywhere,) * 3,
+        scratch_shapes=[pltpu.VMEM(*s) for s in shapes]
+        + [pltpu.SemaphoreType.DMA((10,)), pltpu.SemaphoreType.DMA((10,))],
+        compiler_params=pltpu.CompilerParams(vmem_limit_bytes=62 * MIB),
+        name="place",
+    )(*arrays)
+
+
 def local(
     cotangent,
     decoder_kernel,
@@ -798,7 +833,7 @@
     adapter_down_rows,
     adapter_up_rows,
 ):
-    pre_grad, up_grad, down_grad = main(
+    parts = main(
         cotangent[0],
         decoder_kernel.transpose(1, 2, 0).reshape(144, 512),
         stored_hidden_state,
@@ -810,6 +845,7 @@
         output_norm_scale,
         output_gate,
     )
+    pre_grad, up_grad, down_grad = place(*parts)
     return pre_grad, up_grad.T, down_grad.T
 
 

time: 55.3 us -> 53.2 us (0.962)
  the two profiles are of different devices: /device:TPU:1 before, /device:TPU:9 now
where the time goes in v4:
time: 53.2 us; the launch traced here: 53.1 us
  Pallas kernels  52.3 us (98%)
  between operations  0.82 us (2%)
    pallas_call x1, Pallas kernels, main(): pl.pallas_call(main_kernel, out_shape=(jax.ShapeDtypeStruct((4, 256, F),...  49.4 us
    pallas_call x1, Pallas kernels, place(): pl.pallas_call(place_kernel, out_shape=tuple((jax.ShapeDtypeStruct(*s) fo...  2.84 us

profile of v4, /device:TPU:9, one launch (start us, length us, event | category | flops | bytes accessed | tf_op | source)
XLA Modules:
  0.0 53.1 jit_solution(6930525470550406406)
XLA Ops:
  0.6 49.4 %main.1 = (bf16[4,256,1536]{2,1,0:T(8,128)(2,1)}, f32[64,192]{1,0:T(8,128)}, f32[64,96]{1,0:T(8,128)}) custom-call(bf16[16,128,128]{2,1,0:T(8,128)(2,1)} %bitcast.7, bf16[144,512]{1,0:T(8,128)(2,1)} %bitcast.9, bf16[4,256,3072]{2,1,0:T(8,128)(2,1)} %stored.1, bf16[4,256,1536]{2,1,0:T(8,128)(2,1)} %pre.1, bf16[1536,3072]{1,0:T(8,128)(2,1)} %weight.1, ...), custom_call_target="tpu_custom_call" | custom-call | tf_op jit(solution)/shard_map/main/pallas_call | solution.py:701
  50.1 2.8 %place.1 = (bf16[4,256,1536]{2,1,0:T(8,128)(2,1)}, f32[64,192]{1,0:T(8,128)}, f32[64,96]{1,0:T(8,128)}) custom-call(bf16[4,256,1536]{2,1,0:T(8,128)(2,1)} %get-tuple-element.9.pre, f32[64,192]{1,0:T(8,128)} %get-tuple-element.10.up, f32[64,96]{1,0:T(8,128)} %get-tuple-element.11.down), custom_call_target="tpu_custom_call" | custom-call | tf_op jit(solution)/shard_map/place/pallas_call | solution.py:812

commit v5 on v4

--- a/solution.py
+++ b/solution.py
@@ -258,6 +258,7 @@
                     )
 
     conv(1 - core, dbuf)
+    conv(core, own)
     pl.semaphore_wait(barrier, 46 - c_self.astype(jnp.int32) - e_self.astype(jnp.int32))
 
     copy_a = pltpu.make_async_remote_copy(
@@ -269,16 +270,32 @@
         device_id_type=MESH,
     )
     copy_a.start()
-    conv(core, own)
     for copy in small[2:]:
         copy.wait()
+
+    def all_of(ref, count, send, got):
+        some = ref.at[pl.ds(0, count)]
+        return pltpu.make_async_remote_copy(
+            src_ref=some,
+            dst_ref=some,
+            send_sem=send.at[0],
+            recv_sem=got.at[0],
+            device_id=(w, lax.rem(n + 1, 8)),
+            device_id_type=MESH,
+        )
+
+    def sum_of(ref, count):
+        acc = ref[0]
+        for k in range(1, count):
+            acc = acc + ref[k]
+        return acc
 
     def copy_b(src, slot, t, dev):
         return pltpu.make_async_remote_copy(
             src_ref=own.at[src],
             dst_ref=recv_b.at[slot],
-            send_sem=send_b.at[t],
-            recv_sem=got_b.at[slot],
+            send_sem=send_b.at[0],
+            recv_sem=got_b.at[0],
             device_id=dev,
             device_id_type=MESH,
         )
@@ -391,8 +408,8 @@
         return pltpu.make_async_remote_copy(
             src_ref=low_part.at[t],
             dst_ref=recv_l.at[slot],
-            send_sem=send_l.at[t],
-            recv_sem=got_l.at[slot],
+            send_sem=send_l.at[0],
+            recv_sem=got_l.at[0],
             device_id=(w, t),
             device_id_type=MESH,
         )
@@ -429,21 +446,16 @@
         return pltpu.make_async_remote_copy(
             src_ref=red,
             dst_ref=recv_c.at[slot],
-            send_sem=send_c.at[dn],
-            recv_sem=got_c.at[slot],
+            send_sem=send_c.at[0],
+            recv_sem=got_c.at[0],
             device_id=(c_wide, dn),
             device_id_type=MESH,
         )
 
     my_c_slot = 2 * img + lax.rem(n, 2)
-    total = own[me_b]
-    red[...] = total
-
-    @pl.loop(1, 16)
-    def _(k):
-        t = lax.rem(me_b + k, 16)
-        copy_b(t, t, t, b_device(t)).wait_recv()
-        red[...] += recv_b[t]
+    recv_b[me_b] = own[me_b]
+    all_of(recv_b, 15, send_b, got_b).wait_recv()
+    red[...] = sum_of(recv_b, 16)
 
     @pl.loop(1, 9)
     def _(k):
@@ -461,20 +473,15 @@
         return pltpu.make_async_remote_copy(
             src_ref=red_l,
             dst_ref=recv_m.at[slot],
-            send_sem=send_m.at[t],
-            recv_sem=got_m.at[slot],
+            send_sem=send_m.at[0],
+            recv_sem=got_m.at[0],
             device_id=(w, t),
             device_id_type=MESH,
         )
 
-    red_l[...] = low_part[n]
-
-    @pl.loop(1, 8)
-    def _(k):
-        t = lax.rem(n + k, 8)
-        copy_l(t, t).wait_recv()
-        red_l[...] += recv_l[t]
-
+    recv_l[n] = low_part[n]
+    all_of(recv_l, 7, send_l, got_l).wait_recv()
+    red_l[...] = sum_of(recv_l, 8)
     recv_m[n] = red_l[...]
 
     @pl.loop(1, 8)
@@ -491,18 +498,15 @@
     small_products(3, sums)
     put = dot_nt(u_ref[...], pc[...])
 
-    @pl.loop(0, 8)
-    def _(k):
-        sw, sn = 4 * lax.div(k, 2) + grp, 2 * img + lax.rem(k, 2)
-
-        @pl.when(jnp.logical_or(sw != w, sn != n))
-        def _():
-            copy_c(0, k).wait_recv()
-
-    @pl.loop(1, 8)
-    def _(k):
-        t = lax.rem(n + k, 8)
-        copy_m(t, t).wait_recv()
+    @pl.when(c_self)
+    def _():
+        all_of(recv_c, 7, send_c, got_c).wait_recv()
+
+    @pl.when(jnp.logical_not(c_self))
+    def _():
+        all_of(recv_c, 8, send_c, got_c).wait_recv()
+
+    all_of(recv_m, 7, send_m, got_m).wait_recv()
 
     t1 = []
     for i in range(4):
@@ -541,8 +545,8 @@
         return pltpu.make_async_remote_copy(
             src_ref=ubuf.at[lax.div(t, 8), pl.ds(pl.multiple_of(lax.rem(t, 8) * 8, 8), 8)],
             dst_ref=recv_u.at[slot],
-            send_sem=send_u.at[t],
-            recv_sem=got_u.at[slot],
+            send_sem=send_u.at[0],
+            recv_sem=got_u.at[0],
             device_id=(t, n),
             device_id_type=MESH,
         )
@@ -566,8 +570,8 @@
         return pltpu.make_async_remote_copy(
             src_ref=dbuf.at[t],
             dst_ref=recv_d.at[slot],
-            send_sem=send_d.at[t],
-            recv_sem=got_d.at[slot],
+            send_sem=send_d.at[0],
+            recv_sem=got_d.at[0],
             device_id=(t, n),
             device_id_type=MESH,
         )
@@ -584,20 +588,16 @@
         return pltpu.make_async_remote_copy(
             src_ref=red_u,
             dst_ref=recv_e.at[slot],
-            send_sem=send_e.at[dn],
-            recv_sem=got_e.at[slot],
+            send_sem=send_e.at[0],
+            recv_sem=got_e.at[0],
             device_id=(e_wide, dn),
             device_id_type=MESH,
         )
 
     my_e_slot = lax.rem(w, 8)
-    red_u[...] = ubuf[lax.div(w, 8), pl.ds(pl.multiple_of(my_e_slot * 8, 8), 8)]
-
-    @pl.loop(1, 16)
-    def _(k):
-        t = lax.rem(w + k, 16)
-        copy_u(t, t).wait_recv()
-        red_u[...] += recv_u[t]
+    recv_u[w] = ubuf[lax.div(w, 8), pl.ds(pl.multiple_of(my_e_slot * 8, 8), 8)]
+    all_of(recv_u, 15, send_u, got_u).wait_recv()
+    red_u[...] = sum_of(recv_u, 16)
 
     @pl.loop(1, 9)
     def _(k):
@@ -643,50 +643,41 @@
         out_copy(i).start()
 
     recv_d[w] = dbuf[w]
-
-    @pl.loop(1, 16)
-    def _(k):
-        t = lax.rem(w + k, 16)
-        copy_d(t, t).wait_recv()
-
-    down = recv_d[0]
-    for t in range(1, 16):
-        down = down + recv_d[t]
-    down_out[...] = down[:, :96]
-
-    @pl.loop(0, 8)
-    def _(k):
-        @pl.when(jnp.logical_or(8 * core + k != w, lax.div(w, 2) != n))
-        def _():
-            copy_e(0, k).wait_recv()
+    all_of(recv_d, 15, send_d, got_d).wait_recv()
+    down_out[...] = sum_of(recv_d, 16)[:, :96]
+
+    @pl.when(e_self)
+    def _():
+        all_of(recv_e, 7, send_e, got_e).wait_recv()
+
+    @pl.when(jnp.logical_not(e_self))
+    def _():
+        all_of(recv_e, 8, send_e, got_e).wait_recv()
 
     up = jnp.concatenate([recv_e[k] for k in range(8)], 0)
     up_out[...] = up[:, :192]
 
-    @pl.loop(1, 16)
-    def _(k):
-        t = lax.rem(me_b + k, 16)
-        copy_b(t, t, t, b_device(t)).wait_send()
-        t = lax.rem(w + k, 16)
-        copy_u(t, t).wait_send()
-        copy_d(t, t).wait_send()
-
-    @pl.loop(1, 9)
-    def _(k):
-        dn = lax.rem(n + k, 8)
-
-        @pl.when(k < 8)
-        def _():
-            copy_l(dn, n).wait_send()
-            copy_m(dn, n).wait_send()
-
-        @pl.when(jnp.logical_or(k < 8, jnp.logical_not(c_self)))
-        def _():
-            copy_c(dn, my_c_slot).wait_send()
-
-        @pl.when(jnp.logical_or(k < 8, jnp.logical_not(e_self)))
-        def _():
-            copy_e(dn, my_e_slot).wait_send()
+    all_of(recv_b, 15, send_b, got_b).wait_send()
+    all_of(recv_l, 7, send_l, got_l).wait_send()
+    all_of(recv_m, 7, send_m, got_m).wait_send()
+    all_of(recv_u, 15, send_u, got_u).wait_send()
+    all_of(recv_d, 15, send_d, got_d).wait_send()
+
+    @pl.when(c_self)
+    def _():
+        all_of(recv_c, 7, send_c, got_c).wait_send()
+
+    @pl.when(jnp.logical_not(c_self))
+    def _():
+        all_of(recv_c, 8, send_c, got_c).wait_send()
+
+    @pl.when(e_self)
+    def _():
+        all_of(recv_e, 7, send_e, got_e).wait_send()
+
+    @pl.when(jnp.logical_not(e_self))
+    def _():
+        all_of(recv_e, 8, send_e, got_e).wait_send()
 
     @pl.loop(0, 4)
     def _(i):
@@ -762,20 +753,20 @@
             dma((4,)),
             dma((1,)),
             dma((1,)),
-            dma((16,)),
-            dma((16,)),
-            dma((8,)),
-            dma((8,)),
-            dma((8,)),
-            dma((8,)),
-            dma((8,)),
-            dma((8,)),
-            dma((16,)),
-            dma((16,)),
-            dma((8,)),
-            dma((8,)),
-            dma((16,)),
-            dma((16,)),
+            dma((1,)),
+            dma((1,)),
+            dma((1,)),
+            dma((1,)),
+            dma((1,)),
+            dma((1,)),
+            dma((1,)),
+            dma((1,)),
+            dma((1,)),
+            dma((1,)),
+            dma((1,)),
+            dma((1,)),
+            dma((1,)),
+            dma((1,)),
         ],
         compiler_params=pltpu.CompilerParams(
             collective_id=0, has_side_effects=True, vmem_limit_bytes=62 * MIB

time: 53.2 us -> 53 us (level)
  the two profiles are of different devices: /device:TPU:9 before, /device:TPU:1 now
where the time goes in v5:
time: 53 us; the launch traced here: 52.9 us
  Pallas kernels  52.1 us (98%)
  between operations  0.82 us (2%)
    pallas_call x1, Pallas kernels, main(): pl.pallas_call(main_kernel, out_shape=(jax.ShapeDtypeStruct((4, 256, F),...  49.2 us
    pallas_call x1, Pallas kernels, place(): pl.pallas_call(place_kernel, out_shape=tuple((jax.ShapeDtypeStruct(*s) fo...  2.84 us

profile of v5, /device:TPU:1, one launch (start us, length us, event | category | flops | bytes accessed | tf_op | source)
XLA Modules:
  0.0 52.9 jit_solution(15114446035166585354)
XLA Ops:
  0.6 49.2 %main.1 = (bf16[4,256,1536]{2,1,0:T(8,128)(2,1)}, f32[64,192]{1,0:T(8,128)}, f32[64,96]{1,0:T(8,128)}) custom-call(bf16[16,128,128]{2,1,0:T(8,128)(2,1)} %bitcast.7, bf16[144,512]{1,0:T(8,128)(2,1)} %bitcast.9, bf16[4,256,3072]{2,1,0:T(8,128)(2,1)} %stored.1, bf16[4,256,1536]{2,1,0:T(8,128)(2,1)} %pre.1, bf16[1536,3072]{1,0:T(8,128)(2,1)} %weight.1, ...), custom_call_target="tpu_custom_call" | custom-call | tf_op jit(solution)/shard_map/main/pallas_call | solution.py:692
  49.9 2.8 %place.1 = (bf16[4,256,1536]{2,1,0:T(8,128)(2,1)}, f32[64,192]{1,0:T(8,128)}, f32[64,96]{1,0:T(8,128)}) custom-call(bf16[4,256,1536]{2,1,0:T(8,128)(2,1)} %get-tuple-element.9.pre, f32[64,192]{1,0:T(8,128)} %get-tuple-element.10.up, f32[64,96]{1,0:T(8,128)} %get-tuple-element.11.down), custom_call_target="tpu_custom_call" | custom-call | tf_op jit(solution)/shard_map/place/pallas_call | solution.py:803

commit v6 on v5

--- a/solution.py
+++ b/solution.py
@@ -366,8 +366,8 @@
         acc = lax.fori_loop(0, 24, fill, jnp.zeros((128, 128), F32), unroll=24)
         return jnp.sum(acc, axis=1, keepdims=True)
 
-    def large(i):
-        nz[256 * i : 256 * i + 256, :] = dot_nt(zps[i][...], weight_v[...])
+    def large(i, first=0, last=F):
+        nz[256 * i : 256 * i + 256, first:last] = dot_nt(zps[i][...], weight_v[first:last, :])
 
     def small_products(i, sums):
         tokens = slice(256 * i, 256 * i + 256)
@@ -496,6 +496,7 @@
     slopes(0)
     slopes(1)
     small_products(3, sums)
+    large(3, 0, F // 2)
     put = dot_nt(u_ref[...], pc[...])
 
     @pl.when(c_self)
@@ -580,7 +581,7 @@
     def _(k):
         copy_d(lax.rem(w + k, 16), w).start()
 
-    large(3)
+    large(3, F // 2, F)
     slopes(2)
     slopes(3)
 

time: 53 us -> 53.4 us (level)
  no operation moved by 1% of the time
where the time goes in v6:
time: 53.4 us; the launch traced here: 53.2 us
  Pallas kernels  52.4 us (98%)
  between operations  0.82 us (2%)
    pallas_call x1, Pallas kernels, main(): pl.pallas_call(main_kernel, out_shape=(jax.ShapeDtypeStruct((4, 256, F),...  49.6 us
    pallas_call x1, Pallas kernels, place(): pl.pallas_call(place_kernel, out_shape=tuple((jax.ShapeDtypeStruct(*s) fo...  2.84 us

profile of v6, /device:TPU:1, one launch (start us, length us, event | category | flops | bytes accessed | tf_op | source)
XLA Modules:
  0.0 53.2 jit_solution(4361694240641721730)
XLA Ops:
  0.6 49.6 %main.1 = (bf16[4,256,1536]{2,1,0:T(8,128)(2,1)}, f32[64,192]{1,0:T(8,128)}, f32[64,96]{1,0:T(8,128)}) custom-call(bf16[16,128,128]{2,1,0:T(8,128)(2,1)} %bitcast.7, bf16[144,512]{1,0:T(8,128)(2,1)} %bitcast.9, bf16[4,256,3072]{2,1,0:T(8,128)(2,1)} %stored.1, bf16[4,256,1536]{2,1,0:T(8,128)(2,1)} %pre.1, bf16[1536,3072]{1,0:T(8,128)(2,1)} %weight.1, ...), custom_call_target="tpu_custom_call" | custom-call | tf_op jit(solution)/shard_map/main/pallas_call | solution.py:693
  50.2 2.8 %place.1 = (bf16[4,256,1536]{2,1,0:T(8,128)(2,1)}, f32[64,192]{1,0:T(8,128)}, f32[64,96]{1,0:T(8,128)}) custom-call(bf16[4,256,1536]{2,1,0:T(8,128)(2,1)} %get-tuple-element.9.pre, f32[64,192]{1,0:T(8,128)} %get-tuple-element.10.up, f32[64,96]{1,0:T(8,128)} %get-tuple-element.11.down), custom_call_target="tpu_custom_call" | custom-call | tf_op jit(solution)/shard_map/place/pallas_call | solution.py:804
